TPU v7x, 256 devices: a whole 4x4x8 slice. The times are simulated.
256 devices in a mesh: lon: 64 (over x_hi, y, z), dp: 4 (over x_lo, core).
Axes of the slice: x: 4 (x_hi: 2, x_lo: 2; x = x_hi * 2 + x_lo), y: 4, z: 8, core: 2. Of those that a mesh axis runs over, the one named last changes fastest.
Arguments:
- fields: bfloat16 [4, 77, 512, 128], P('dp', None, 'lon'), may hold values from -6 to 6
- targets: bfloat16 [4, 77, 512, 128], P('dp', None, 'lon'), as said below
- land_sea: int32 [512, 128], P('lon'), may hold values 0 or 1
- clip_level: int32 [77], replicated, may hold values from 2 to 63
- stem_weight: bfloat16 [200, 77], P('dp'), may hold values from -0.625 to 0.625
- dw_kernel: bfloat16 [200, 49], P('dp'), may hold values from -0.875 to 0.875
- up_weight: bfloat16 [200, 800], P('dp'), may hold values from -0.4375 to 0.4375
- down_weight: bfloat16 [800, 200], P('dp'), may hold values from -0.21875 to 0.21875
- head_weight: bfloat16 [200, 77], P('dp'), may hold values from -0.4375 to 0.4375
Outputs:
- stem_weight_gradient: float32 [200, 77], P('dp')
- grad_kernel: float32 [200, 49], P('dp')
- grad_up: float32 [200, 800], P('dp')
- grad_down: float32 [800, 200], P('dp')
- grad_head: float32 [200, 77], P('dp')
- loss: float32 [], replicated
- field_sensitivity: float32 [4, 77, 512, 128], P('dp', None, 'lon')
Inputs may be any that keep to these rules, and one draw needn't show every extreme that they name: targets are real-valued ocean fields between -8 and 8.
All inputs are finite; a program needn't handle non-finite values. No bound on the sum of `land_sea` on one device may be relied on, other than what follows from the above.
Results may differ from a plain program's by a relative error of at most 0.011.
Values may be sent and summed in bfloat16 or wider, within the bound.
A program may use at most 64 MiB of HBM per device.

v0:
```python
import jax
import jax.numpy as jnp
from jax import lax
from jax.experimental import pallas as pl
from jax.experimental.pallas import tpu as pltpu
from jax.sharding import PartitionSpec as P

MESH = pl.DeviceIdType.MESH
F32 = jnp.float32
BF16 = jnp.bfloat16

V = 77
VP = 80
C = 200
CP = 256
FF = 800
FP = 896
FB = 160
COLS = 8
LAT = 128
SIDE = 7
HALO = 6
SLOTS = COLS + 2 * HALO
CELLS = COLS * LAT
GELU_K = 0.7978845608


def dot(a, b):
    return jnp.dot(a, b, preferred_element_type=F32)


def dot_nt(a, b):
    return lax.dot_general(a, b, (((1,), (1,)), ((), ())), preferred_element_type=F32)


def remote(src, dst, send, recv, device):
    return pltpu.make_async_remote_copy(
        src_ref=src,
        dst_ref=dst,
        send_sem=send,
        recv_sem=recv,
        device_id=device,
        device_id_type=MESH,
    )


def padded_row(channel):
    step = (channel >= 50).astype(jnp.int32)
    step += (channel >= 100).astype(jnp.int32)
    step += (channel >= 150).astype(jnp.int32)
    return channel + 14 * step


def body(*refs):
    inputs, outputs, rest = refs[:9], refs[9:16], refs[16:]
    held, made = rest[:9], rest[9:16]
    o_stem, o_kern, o_up, o_down, o_head, o_loss, o_sens = made
    fields, targets, land, clip, stem, dw, up, down, head = held
    (
    f32a, f32b, fbuf, fm, wp, wd, ga, gb, gd,
        stem_w, stem_t, up_w, up_t, head_w, head_t, down_w, down_t, down_f,
        taps, corrs, xs, ms, nh, nhp, act, slope, pre, bo, mis, limits, sq, sa, sb,
        bg, bh, gdn, gup, back, sh, small, smp,
        ld, lu, rd0, ru0, ls_d, ls_u, rx_d, rx_u, part_large, lg,
        stx, srx, s2x, sfin, sen, hl, hr, cells,
        send_g, recv_g, send_h, recv_h, send_s, recv_s, load_sem, store_sem,
    ) = rest[16:]
    lon = lax.axis_index("lon")
    dp = lax.axis_index("dp")
    x_hi, y, z = lon // 32, (lon // 8) % 4, lon % 8
    x_lo, core = dp // 2, dp % 2
    right = ((lon + 1) % 64, dp)
    left = ((lon + 63) % 64, dp)
    sibling = (lon, x_lo * 2 + (1 - core))
    idx_p = (x_hi * 4 + y) * 4 + dp
    idx_m = (x_lo * 4 + y) * 2 + x_hi
    idx_h = x_hi * 4 + y

    def peer_p(k):
        j = (idx_p + k) % 32
        return j, ((j // 4) * 8 + z, j % 4)

    def peer_z(k):
        j = (z + k) % 8
        return j, (x_hi * 32 + y * 8 + j, dp)

    def peer_m(k):
        j = (idx_m + k) % 16
        return j, ((j % 2) * 32 + ((j // 2) % 4) * 8 + z, (j // 8) * 2 + core)

    def peer_h(k):
        j = (idx_h + k) % 8
        return j, (j * 8 + z, dp)

    loads = [
        pltpu.make_async_copy(src, dst, load_sem.at[n])
        for n, (src, dst) in enumerate(zip(inputs, held))
    ]
    for copy in loads:
        copy.start()
    stores = [
        pltpu.make_async_copy(src, dst, store_sem.at[n])
        for n, (src, dst) in enumerate(zip(made, outputs))
    ]

    barrier = pltpu.get_barrier_semaphore()
    for target in (right, left):
        pl.semaphore_signal(barrier, inc=1, device_id=target, device_id_type=MESH)
    for k in range(1, 32):
        pl.semaphore_signal(barrier, inc=1, device_id=peer_p(k)[1], device_id_type=MESH)
    for k in range(1, 8):
        pl.semaphore_signal(barrier, inc=1, device_id=peer_z(k)[1], device_id_type=MESH)

    for copy in loads:
        copy.wait()
    f32a[0 : V * COLS, :] = fields[...].astype(F32).reshape(V * COLS, LAT)
    f32a[V * COLS : VP * COLS, :] = jnp.zeros(((VP - V) * COLS, LAT), F32)
    f32b[0 : V * COLS, :] = targets[...].astype(F32).reshape(V * COLS, LAT)
    f32b[V * COLS : VP * COLS, :] = jnp.zeros(((VP - V) * COLS, LAT), F32)
    for i in range(COLS):
        fbuf[HALO + i] = f32a[pl.ds(i, VP, stride=COLS), :].astype(BF16)
    wp[...] = jnp.zeros(wp.shape, F32)
    wp[0:50, 0:V] = stem[...].astype(F32)
    wp[0:50, 128:177] = dw[...].astype(F32)
    wp[0:50, 256 : 256 + FF] = up[...].astype(F32)
    wp[0:50, 256 + FP : 256 + FP + V] = head[...].astype(F32)
    wd[...] = jnp.zeros(wd.shape, F32)
    wd[0:C, 0:C] = down[...].astype(F32)
    ga[dp] = wp[:, 0:256].astype(BF16)
    gb[dp] = wp[:, 256 : 256 + FP + 128].astype(BF16)
    gd[dp] = wd[...].astype(BF16)

    pl.semaphore_wait(barrier, 40)

    halo = [
        remote(fbuf.at[pl.ds(8, 6)], fbuf.at[pl.ds(0, 6)], send_h.at[0], recv_h.at[0], right),
        remote(fbuf.at[pl.ds(6, 6)], fbuf.at[pl.ds(14, 6)], send_h.at[1], recv_h.at[1], left),
    ]
    first_weights = [
        remote(ga.at[dp], ga.at[dp], send_g.at[k - 1], recv_g.at[k - 1], (lon, (dp + k) % 4))
        for k in range(1, 4)
    ]
    for copy in first_weights:
        copy.start()
    across = (lon, (1 - x_lo) * 2 + core)
    far = (1 - x_lo) * 2 + core
    large_weights = []
    for a, buf in enumerate((gb, gd)):
        at = 3 + 3 * a
        large_weights.append(
            (
                remote(buf.at[dp], buf.at[dp], send_g.at[at], recv_g.at[at], across),
                remote(buf.at[dp], buf.at[dp], send_g.at[at + 1], recv_g.at[at + 1], sibling),
                remote(buf.at[far], buf.at[far], send_g.at[at + 2], recv_g.at[at + 2], sibling),
            )
        )

    def pass_on(a):
        large_weights[a][0].wait_recv()
        large_weights[a][2].start()

    pending = []

    def stage(index, count, peers, src, dst):
        for k in range(1, count):
            j, device = peers(k)
            remote(src(j), dst, send_s.at[index], recv_s.at[index], device).start()

    def stage_wait(index, count, buf):
        whole = buf.at[pl.ds(0, count - 1)]
        both = remote(whole, whole, send_s.at[index], recv_s.at[index], right)
        both.wait_recv()
        pending.append(both)

    row = lax.broadcasted_iota(jnp.int32, (CP, CP), 0)
    col = lax.broadcasted_iota(jnp.int32, (CP, CP), 1)
    from_padded = jnp.where((row < C) & (col == padded_row(row)), 1.0, 0.0).astype(BF16)
    to_padded = jnp.where((col < C) & (row == padded_row(col)), 1.0, 0.0).astype(BF16)
    lane = lax.broadcasted_iota(jnp.int32, (8, LAT), 1)
    keep = {b: (lane + b >= 0) & (lane + b < LAT) for b in range(-HALO, HALO + 1, 2)}

    for i in range(COLS):
        fm[:, (HALO + i) * LAT : (HALO + i + 1) * LAT] = fbuf[HALO + i]

    for copy in halo:
        copy.start()
    for copy in first_weights:
        copy.wait_recv()
    large_weights[0][0].start()
    large_weights[0][1].start()
    large_weights[1][1].start()
    first = dot(from_padded, ga[...].reshape(CP, 256))
    stem_w[...] = first[:, 0:128].astype(BF16)
    stem_t[...] = first[:, 0:128].T.astype(BF16)
    def stem_pair(s):
        out = dot(stem_w[:, 0:VP], fm[:, s * LAT : (s + 2) * LAT])[0:C].astype(BF16).astype(F32)
        xs[s] = out[:, 0:LAT]
        xs[s + 1] = out[:, LAT : 2 * LAT]

    for s in range(HALO, HALO + COLS, 2):
        stem_pair(s)
    kern_w = first[0:C, 128:256].astype(BF16)
    tap_row = lax.broadcasted_iota(jnp.int32, (LAT, 2 * LAT), 0)
    second_half = (lax.broadcasted_iota(jnp.int32, (LAT, 2 * LAT), 1) >= LAT).astype(jnp.int32)
    for t in range(0, SIDE * SIDE, 2):
        spread = dot(kern_w, jnp.where(tap_row == t + second_half, 1.0, 0.0).astype(BF16))
        taps[t] = spread[:, 0:LAT]
        if t + 1 < SIDE * SIDE:
            taps[t + 1] = spread[:, LAT : 2 * LAT]
    for copy in halo:
        copy.wait_recv()
    for s in list(range(0, HALO)) + list(range(HALO + COLS, SLOTS)):
        fm[:, s * LAT : (s + 1) * LAT] = fbuf[s]
    for s in list(range(0, HALO, 2)) + list(range(HALO + COLS, SLOTS, 2)):
        stem_pair(s)

    def conv_forward(block, carry):
        here = pl.ds(pl.multiple_of(block * 8, 8), 8)
        for first_col in (0, 4):
            x = [xs[first_col + s, here, :] for s in range(4 + 2 * HALO)]
            out = [None] * 4
            for q in range(SIDE):
                b = (q - 3) * 2
                w = [taps[p * SIDE + q, here, :] for p in range(SIDE)]
                for i in range(4):
                    total = w[0] * x[i]
                    for p in range(1, SIDE):
                        total = total + w[p] * x[i + 2 * p]
                    if b != 0:
                        total = jnp.where(keep[b], pltpu.roll(total, (-b) % LAT, 1), 0.0)
                    out[i] = total if out[i] is None else out[i] + total
            for i in range(4):
                ms[first_col + i, here, :] = out[i]
        return carry

    lax.fori_loop(0, 13, conv_forward, 0)
    pass_on(0)
    large_weights[1][0].start()
    lax.fori_loop(13, C // 8, conv_forward, 0)

    nh[...] = jnp.zeros(nh.shape, BF16)
    rstds = []
    for i in range(COLS):
        tile = ms[i]
        centred = tile - jnp.mean(tile, axis=0, keepdims=True)
        rstd = lax.rsqrt(jnp.mean(centred * centred, axis=0, keepdims=True) + 1e-06)
        normed = centred * rstd
        ms[i] = normed
        rstds.append(rstd)
        nh[0:C, i * LAT : (i + 1) * LAT] = normed.astype(BF16)

    large_weights[0][1].wait_recv()
    large_weights[0][2].wait_recv()
    second = dot(from_padded, gb[...].reshape(CP, FP + 128))
    up_w[...] = second[:, 0:FP].astype(BF16)
    up_t[...] = second[:, 0:FP].T.astype(BF16)
    head_w[...] = second[:, FP : FP + 128]
    head_t[...] = second[:, FP : FP + 128].T.astype(BF16)
    limits[...] = jnp.ones((1, LAT), F32)
    limits[:, 0:V] = clip[...].astype(F32) / 16.0
    sq[...] = jnp.zeros(sq.shape, F32)
    bo[...] = jnp.zeros(bo.shape, BF16)
    for j in range(0, 2):
        part = pl.ds(j * 2 * LAT, 2 * LAT)
        for f in range(0, FF, FB):
            u = dot(up_t[f : f + FB, :], nh[:, part])
            u2 = u * u
            half = 0.5 + 0.5 * jnp.tanh(u * (GELU_K + (GELU_K * 0.044715) * u2))
            value = u * half
            act[f : f + FB, part] = value.astype(BF16)
            slope[f : f + FB, part] = half + value * (1.0 - half) * (
                2.0 * GELU_K + (6.0 * GELU_K * 0.044715) * u2
            )
    pass_on(1)
    for j in range(2, 4):
        part = pl.ds(j * 2 * LAT, 2 * LAT)
        for f in range(0, FF, FB):
            u = dot(up_t[f : f + FB, :], nh[:, part])
            u2 = u * u
            half = 0.5 + 0.5 * jnp.tanh(u * (GELU_K + (GELU_K * 0.044715) * u2))
            value = u * half
            act[f : f + FB, part] = value.astype(BF16)
            slope[f : f + FB, part] = half + value * (1.0 - half) * (
                2.0 * GELU_K + (6.0 * GELU_K * 0.044715) * u2
            )
    large_weights[1][1].wait_recv()
    large_weights[1][2].wait_recv()
    for d in range(4):
        down_f[C * d : C * (d + 1), :] = gd[d].astype(F32)[0:C]
    down_w[...] = down_f[...].astype(BF16)
    down_t[...] = down_f[...].T.astype(BF16)

    for j in range(COLS // 2):
        part = pl.ds(j * 2 * LAT, 2 * LAT)
        branch = dot(down_t[...], act[:, part])[0:C]
        centre = jnp.concatenate([xs[HALO + 2 * j], xs[HALO + 2 * j + 1]], axis=1)
        bo[0:C, part] = (centre + branch).astype(BF16)
    for j in range(COLS // 2):
        part = pl.ds(j * 2 * LAT, 2 * LAT)
        predicted = dot(head_t[0:VP, :], bo[:, part])
        for h in range(2):
            i = 2 * j + h
            ocean = land[i : i + 1, :].astype(F32)
            wanted = f32b[pl.ds(i, VP, stride=COLS), :]
            miss = (predicted[:, h * LAT : (h + 1) * LAT] - wanted) * ocean
            mis[:, i * LAT : (i + 1) * LAT] = miss.astype(BF16)
            sq[0:VP, :] = sq[0:VP, :] + miss * miss

    lanes = lax.broadcasted_iota(jnp.int32, (1, LAT), 1)
    ocean_local = jnp.sum(land[...].astype(F32))
    mine = jnp.sum(sq[...].T, axis=0, keepdims=True)
    sa[idx_p] = jnp.where(lanes == V, ocean_local, mine)
    stage(0, 32, peer_p, lambda j: sa.at[idx_p], sa.at[idx_p])

    nhp[...] = dot(to_padded, nh[...]).astype(BF16)
    small[:, 128:256] = jnp.zeros((CP, 128), F32)
    small[:, 128 : 128 + VP] = dot_nt(bo[...], mis[...])

    stage_wait(0, 32, sa)
    total = sa[0]
    for j in range(1, 32):
        total = total + sa[j]
    sb[z] = total
    stage(1, 8, peer_z, lambda j: sb.at[z], sb.at[z])
    stage_wait(1, 8, sb)
    total = sb[0]
    for j in range(1, 8):
        total = total + sb[j]
    ocean_count = jnp.sum(jnp.where(lanes == V, total, 0.0), axis=1, keepdims=True)
    valid = lanes < V
    threshold = limits[...]
    mean_error = jnp.where(valid, total, 0.0) / ocean_count
    ratio = 1.0 + mean_error / threshold
    o_loss[...] = jnp.sum(jnp.where(valid, threshold * jnp.log(ratio), 0.0), axis=1, keepdims=True)
    stores[5].start()
    factor = jnp.where(valid, 2.0 / (ocean_count * ratio), 0.0)

    small[:, 128:256] = small[:, 128:256] * factor
    scaled = (head_w[...] * factor).astype(BF16)
    for j in range(COLS // 2):
        part = pl.ds(j * 2 * LAT, 2 * LAT)
        grad = dot(scaled[:, 0:VP], mis[:, part])
        bg[:, part] = grad[0:C]
        bh[:, part] = grad.astype(BF16)
    gdn[FF : FF + 64, :] = jnp.zeros((64, CP), F32)
    for f in range(0, FF, FB):
        gdn[f : f + FB, :] = dot_nt(act[f : f + FB, :], bh[...])
    for d in range(4):
        for s in range(4):
            piece = (d % 2) * 16 + (d // 2) * 8 + s * 2
            block = gdn[C * d + 64 * s : C * d + 64 * s + 64, :]
            ld[piece] = block[:, 0:128].astype(BF16)
            ld[piece + 1] = block[:, 128:256].astype(BF16)
    away = pl.ds((1 - core) * 16, 16)
    copy_d = remote(ld.at[away], rd0, send_s.at[2], recv_s.at[2], sibling)
    copy_d.start()

    pre[FF:FP, :] = jnp.zeros((FP - FF, CELLS), BF16)
    for j in range(COLS // 2):
        part = pl.ds(j * 2 * LAT, 2 * LAT)
        for f in range(0, FF, FB):
            pre[f : f + FB, part] = (
                dot(down_w[f : f + FB, :], bh[:, part]) * slope[f : f + FB, part]
            ).astype(BF16)
    gup[...] = dot_nt(nhp[...], pre[...])
    for d in range(4):
        for s in range(4):
            piece = (d % 2) * 16 + (d // 2) * 8 + s * 2
            for l in range(7):
                lu[piece + l // 4, 16 * (l % 4) : 16 * (l % 4) + 16, :] = gup[
                    64 * d + 16 * s : 64 * d + 16 * s + 16, 128 * l : 128 * l + 128
                ].astype(BF16)
            lu[piece + 1, 48:64, :] = jnp.zeros((16, 128), BF16)
    copy_u = remote(lu.at[away], ru0, send_s.at[3], recv_s.at[3], sibling)
    copy_u.start()

    for j in range(COLS // 2):
        part = pl.ds(j * 2 * LAT, 2 * LAT)
        grad = dot(up_w[...], pre[:, part])[0:C]
        for h in range(2):
            i = 2 * j + h
            g = grad[:, h * LAT : (h + 1) * LAT]
            normed = ms[i]
            mean_g = jnp.mean(g, axis=0, keepdims=True)
            mean_gn = jnp.mean(g * normed, axis=0, keepdims=True)
            ms[i] = (rstds[i] * (g - mean_g - normed * mean_gn)).astype(BF16).astype(F32)

    copy_d.wait_recv()
    for j in range(16):
        ls_d[j] = (ld[core * 16 + j].astype(F32) + rd0[j].astype(F32)).astype(BF16)
    stage(4, 16, peer_m, lambda j: ls_d.at[j], rx_d.at[idx_m])
    def conv_backward(block, carry):
        here = pl.ds(pl.multiple_of(block * 8, 8), 8)
        x = [xs[s, here, :] for s in range(SLOTS)]
        m = [ms[i, here, :] for i in range(COLS)]
        out = [None] * SLOTS
        for q in range(SIDE):
            b = (q - 3) * 2
            if b != 0:
                shifted = [jnp.where(keep[-b], pltpu.roll(t, b % LAT, 1), 0.0) for t in m]
            else:
                shifted = m
            for p in range(SIDE):
                t = p * SIDE + q
                w = taps[t, here, :]
                corr = None
                for i in range(COLS):
                    s = i + 2 * p
                    term = w * shifted[i]
                    out[s] = term if out[s] is None else out[s] + term
                    prod = shifted[i] * x[s]
                    corr = prod if corr is None else corr + prod
                corrs[t, here, :] = corr
        for s in range(SLOTS):
            back[s, here, :] = out[s]
        return carry

    lax.fori_loop(0, 3, conv_backward, 0)
    copy_u.wait_recv()
    for j in range(16):
        ls_u[j] = (lu[core * 16 + j].astype(F32) + ru0[j].astype(F32)).astype(BF16)
    stage(11, 16, peer_m, lambda j: ls_u.at[j], rx_u.at[idx_m])
    lax.fori_loop(3, C // 8, conv_backward, 0)
    stage_wait(4, 16, rx_d)
    rx_d[idx_m] = ls_d[idx_m]
    large = rx_d[0].astype(F32)
    for j in range(1, 16):
        large = large + rx_d[j].astype(F32)
    part_large[z, 0:64] = large.astype(BF16)
    stage_wait(11, 16, rx_u)
    rx_u[idx_m] = ls_u[idx_m]
    large = rx_u[0].astype(F32)
    for j in range(1, 16):
        large = large + rx_u[j].astype(F32)
    part_large[z, 64:128] = large.astype(BF16)
    stage(5, 8, peer_z, lambda j: part_large.at[z], part_large.at[z])
    tap_col = lax.broadcasted_iota(jnp.int32, (2 * LAT, LAT), 1)
    lower_half = (lax.broadcasted_iota(jnp.int32, (2 * LAT, LAT), 0) >= LAT).astype(jnp.int32)
    kern = None
    for t in range(0, SIDE * SIDE, 2):
        place = jnp.where(tap_col == V + t + lower_half, 1.0, 0.0).astype(BF16)
        terms = corrs[t].astype(BF16)
        if t + 1 < SIDE * SIDE:
            terms = jnp.concatenate([terms, corrs[t + 1].astype(BF16)], axis=1)
        else:
            place = place[0:LAT]
        part_sum = dot(terms, place)
        kern = part_sum if kern is None else kern + part_sum
    small[0:C, 128:256] = small[0:C, 128:256] + kern

    sh[C:CP, :] = jnp.zeros((CP - C, SLOTS * LAT), BF16)
    for s in range(SLOTS):
        value = back[s]
        if HALO <= s < HALO + COLS:
            value = value + bg[:, (s - HALO) * LAT : (s - HALO + 1) * LAT]
        sh[0:C, s * LAT : (s + 1) * LAT] = value.astype(BF16)
    small[:, 0:128] = jnp.zeros((CP, 128), F32)
    small[:, 0:VP] = dot_nt(sh[...], fm[...])
    smp[...] = dot(to_padded, small[...].astype(BF16)).astype(BF16)
    for d in range(4):
        for s in range(4):
            at = 64 * d + 16 * s
            stx[s * 4 + d] = smp[at : at + 16, 0:128]
            stx[16 + s * 4 + d] = smp[at : at + 16, 128:256]
    stage(6, 32, peer_p, lambda j: stx.at[j], srx.at[idx_p])

    for s in list(range(0, HALO, 2)) + list(range(HALO + COLS, SLOTS, 2)):
        value = dot(stem_t[0:VP, :], sh[:, s * LAT : (s + 2) * LAT]).astype(BF16)
        sen[s if s < HALO else s - COLS] = value[:, 0:LAT]
        sen[s + 1 if s < HALO else s + 1 - COLS] = value[:, LAT : 2 * LAT]
    copy_l = remote(sen.at[pl.ds(0, 6)], hr, send_h.at[2], recv_h.at[2], left)
    copy_r = remote(sen.at[pl.ds(6, 6)], hl, send_h.at[3], recv_h.at[3], right)
    copy_l.start()
    copy_r.start()

    for j in range(COLS // 2):
        s = HALO + 2 * j
        value = dot(stem_t[0:VP, :], sh[:, s * LAT : (s + 2) * LAT])
        cells[2 * j] = value[:, 0:LAT]
        cells[2 * j + 1] = value[:, LAT : 2 * LAT]

    stage_wait(6, 32, srx)
    srx[idx_p] = stx[idx_p]
    tiny = srx[0].astype(F32)
    for j in range(1, 32):
        tiny = tiny + srx[j].astype(F32)
    s2x[z] = tiny.astype(BF16)
    stage(8, 8, peer_z, lambda j: s2x.at[z], s2x.at[z])

    stage_wait(5, 8, part_large)
    large = part_large[0].astype(F32)
    for j in range(1, 8):
        large = large + part_large[j].astype(F32)
    lg[idx_h] = large.astype(BF16)
    stage(9, 8, peer_h, lambda j: lg.at[idx_h], lg.at[idx_h])

    stage_wait(8, 8, s2x)
    tiny = s2x[0].astype(F32)
    for j in range(1, 8):
        tiny = tiny + s2x[j].astype(F32)
    sfin[idx_h] = tiny.astype(BF16)
    stage(10, 8, peer_h, lambda j: sfin.at[idx_h], sfin.at[idx_h])

    copy_l.wait_recv()
    copy_r.wait_recv()
    for i in range(COLS):
        value = cells[i]
        if i >= 2:
            value = value + hr[i - 2].astype(F32)
        if i < 6:
            value = value + hl[i].astype(F32)
        o_sens[pl.ds(i, V, stride=COLS), :] = (value * ocean_count)[0:V]
    stores[6].start()

    stage_wait(9, 8, lg)
    for s in range(4):
        rows = 16 if s < 3 else 2
        for l in range(7):
            width = min(128, FF - 128 * l)
            at = 64 + 16 * (l % 4)
            piece = lg[s + 4 * (l // 4), at : at + 16, :].astype(F32)
            o_up[16 * s : 16 * s + rows, 128 * l : 128 * l + width] = piece[0:rows, 0:width]
        rows = 64 if s < 3 else 8
        o_down[64 * s : 64 * s + rows, 0:128] = lg[s, 0:64, :].astype(F32)[0:rows]
        o_down[64 * s : 64 * s + rows, 128:C] = lg[s + 4, 0:64, :].astype(F32)[0:rows, 0 : C - 128]
    stores[2].start()
    stores[3].start()
    stage_wait(10, 8, sfin)
    for s in range(4):
        rows = 16 if s < 3 else 2
        o_stem[16 * s : 16 * s + rows, :] = sfin[s].astype(F32)[0:rows, 0:V]
        piece = sfin[4 + s].astype(F32)
        o_head[16 * s : 16 * s + rows, :] = piece[0:rows, 0:V]
        o_kern[16 * s : 16 * s + rows, :] = pltpu.roll(piece, LAT - V, 1)[0:rows, 0:49]
    for n in (0, 1, 4):
        stores[n].start()
    for copy in first_weights + halo + list(large_weights[0] + large_weights[1]):
        copy.wait_send()
    for copy in [copy_d, copy_u, copy_l, copy_r] + pending:
        copy.wait_send()
    for copy in stores:
        copy.wait()


def hand_over(*refs):
    ins, outs, held, sems = refs[:7], refs[7:14], refs[14:21], refs[21]
    into = [pltpu.make_async_copy(ins[n], held[n], sems.at[n]) for n in range(7)]
    away = [pltpu.make_async_copy(held[n], outs[n], sems.at[7 + n]) for n in range(7)]
    for copy in into:
        copy.start()
    for n in range(7):
        into[n].wait()
        away[n].start()
    for copy in away:
        copy.wait()


SCRATCH = [
    ((V, COLS, LAT), BF16),
    ((V, COLS, LAT), BF16),
    ((COLS, LAT), jnp.int32),
    ((1, V), jnp.int32),
    ((50, V), BF16),
    ((50, SIDE * SIDE), BF16),
    ((50, FF), BF16),
    ((C, C), BF16),
    ((50, V), BF16),
    ((50, V), F32),
    ((50, SIDE * SIDE), F32),
    ((50, FF), F32),
    ((C, C), F32),
    ((50, V), F32),
    ((1, 1), F32),
    ((V * COLS, LAT), F32),
    ((VP * COLS, LAT), F32),
    ((VP * COLS, LAT), F32),
    ((SLOTS, VP, LAT), BF16),
    ((VP, SLOTS * LAT), BF16),
    ((64, 256 + FP + 128), F32),
    ((208, CP), F32),
    ((4, 64, 256), BF16),
    ((4, 64, FP + 128), BF16),
    ((4, 208, CP), BF16),
    ((CP, 128), BF16),
    ((128, CP), BF16),
    ((CP, FP), BF16),
    ((FP, CP), BF16),
    ((CP, 128), F32),
    ((128, CP), BF16),
    ((FF, CP), BF16),
    ((CP, FF), BF16),
    ((FF, CP), F32),
    ((SIDE * SIDE, C, LAT), F32),
    ((SIDE * SIDE, C, LAT), F32),
    ((SLOTS, C, LAT), F32),
    ((COLS, C, LAT), F32),
    ((CP, CELLS), BF16),
    ((CP, CELLS), BF16),
    ((FF, CELLS), BF16),
    ((FF, CELLS), F32),
    ((FP, CELLS), BF16),
    ((CP, CELLS), BF16),
    ((VP, CELLS), BF16),
    ((1, LAT), F32),
    ((128, LAT), F32),
    ((32, 1, LAT), F32),
    ((8, 1, LAT), F32),
    ((C, CELLS), F32),
    ((CP, CELLS), BF16),
    ((FF + 64, CP), F32),
    ((CP, FP), F32),
    ((SLOTS, C, LAT), F32),
    ((CP, SLOTS * LAT), BF16),
    ((CP, 256), F32),
    ((CP, 256), BF16),
    ((32, 64, 128), BF16),
    ((32, 64, 128), BF16),
    ((16, 64, 128), BF16),
    ((16, 64, 128), BF16),
    ((16, 64, 128), BF16),
    ((16, 64, 128), BF16),
    ((16, 64, 128), BF16),
    ((16, 64, 128), BF16),
    ((8, 128, 128), BF16),
    ((8, 128, 128), BF16),
    ((32, 16, 128), BF16),
    ((32, 16, 128), BF16),
    ((8, 16, 128), BF16),
    ((8, 16, 128), BF16),
    ((12, VP, LAT), BF16),
    ((6, VP, LAT), BF16),
    ((6, VP, LAT), BF16),
    ((COLS, VP, LAT), F32),
]


def shards(
    fields, targets, land_sea, clip_level, stem_weight, dw_kernel, up_weight, down_weight, head_weight
):
    anywhere = pl.BlockSpec(memory_space=pl.ANY)
    dma = pltpu.SemaphoreType.DMA
    shapes = [(50, V), (50, 49), (50, FF), (C, C), (50, V), (1, 1), (V * COLS, LAT)]
    results = [jax.ShapeDtypeStruct(s, F32) for s in shapes]
    made = pl.pallas_call(
        body,
        out_shape=results,
        in_specs=[anywhere] * 9,
        out_specs=[anywhere] * 7,
        scratch_shapes=[pltpu.VMEM(s, t) for s, t in SCRATCH]
        + [dma((n,)) for n in (9, 9, 4, 4, 12, 12, 9, 7)],
        compiler_params=pltpu.CompilerParams(
            collective_id=0, has_side_effects=True, vmem_limit_bytes=58 * 1024 * 1024
        ),
    )(
        fields.reshape(V, COLS, LAT),
        targets.reshape(V, COLS, LAT),
        land_sea,
        clip_level.reshape(1, V),
        stem_weight,
        dw_kernel,
        up_weight,
        down_weight,
        head_weight,
    )
    outs = pl.pallas_call(
        hand_over,
        out_shape=results,
        in_specs=[anywhere] * 7,
        out_specs=[anywhere] * 7,
        scratch_shapes=[pltpu.VMEM(s, F32) for s in shapes] + [dma((14,))],
    )(*made)
    return (
        outs[0], outs[1], outs[2], outs[3], outs[4],
        outs[5].reshape(()),
        outs[6].reshape(1, V, COLS, LAT),
    )


def solution(mesh):
    placed = (
        P("dp", None, "lon", None),
        P("dp", None, "lon", None),
        P("lon", None),
        P(),
        P("dp", None),
        P("dp", None),
        P("dp", None),
        P("dp", None),
        P("dp", None),
    )
    return jax.shard_map(
        shards,
        mesh=mesh,
        in_specs=placed,
        out_specs=(
            P("dp", None),
            P("dp", None),
            P("dp", None),
            P("dp", None),
            P("dp", None),
            P(),
            P("dp", None, "lon", None),
        ),
        check_vma=False,
    )
```

profile of v0, /device:TPU:6, one launch (start us, length us, event | category | flops | bytes accessed | tf_op | source)
XLA Modules:
  0.0 68.0 jit_solution(10222557536651704142)
XLA Ops:
  0.6 64.6 %shard_map.144 = (f32[50,77]{1,0:T(8,128)}, f32[50,49]{1,0:T(8,128)}, f32[50,800]{1,0:T(8,128)}, f32[200,200]{1,0:T(8,128)}, f32[50,77]{1,0:T(8,128)}, /*index=5*/f32[1,1]{1,0:T(1,128)}, f32[616,128]{1,0:T(8,128)}) custom-call(bf16[77,8,128]{2,1,0:T(8,128)(2,1)} %bitcast.5, bf16[77,8,128]{2,1,0:T(8,128)(2,1)} %bitcast.6, s32[8,128]{1,0:T(8,128)} %refs_2_.1, ...), custom_call_target="tpu_custom_call" | custom-call | tf_op jit(solution)/shard_map/pallas_call | solution.py:644
  65.2 2.6 %shard_map.145 = (f32[50,77]{1,0:T(8,128)}, f32[50,49]{1,0:T(8,128)}, f32[50,800]{1,0:T(8,128)}, f32[200,200]{1,0:T(8,128)}, f32[50,77]{1,0:T(8,128)}, /*index=5*/f32[1,1]{1,0:T(1,128)}, f32[616,128]{1,0:T(8,128)}) custom-call(f32[50,77]{1,0:T(8,128)} %get-tuple-element.21.refs_0_, f32[50,49]{1,0:T(8,128)} %get-tuple-element.22.refs_1_, ...), custom_call_target="tpu_custom_call" | custom-call | tf_op jit(solution)/shard_map/pallas_call | solution.py:665
where the time goes:
time: 69.2 us; the launch traced here: 68 us
  Pallas kernels  67.2 us (97%)
  between operations  0.8 us (1%)
    pallas_call x1, Pallas kernels, shards(): pl.pallas_call(body, out_shape=results, in_specs=[anywhere] * 9, out_spec...  64.6 us
    pallas_call x1, Pallas kernels, shards(): pl.pallas_call(hand_over, out_shape=results, in_specs=[anywhere] * 7, out...  2.62 us

commit v1 on v0

--- a/solution.py
+++ b/solution.py
@@ -52,19 +52,19 @@
 
 
 def body(*refs):
-    inputs, outputs, rest = refs[:9], refs[9:16], refs[16:]
-    held, made = rest[:9], rest[9:16]
+    inputs, made, rest = refs[:9], refs[9:16], refs[16:]
+    held = rest[:9]
     o_stem, o_kern, o_up, o_down, o_head, o_loss, o_sens = made
     fields, targets, land, clip, stem, dw, up, down, head = held
     (
     f32a, f32b, fbuf, fm, wp, wd, ga, gb, gd,
-        stem_w, stem_t, up_w, up_t, head_w, head_t, down_w, down_t, down_f,
+        stem_w, stem_t, up_w, up_t, head_w, head_s, head_t, down_w, down_t, down_f,
         taps, corrs, xs, ms, nh, nhp, act, slope, pre, bo, mis, limits, sq, sa, sb,
-        bg, bh, gdn, gup, back, sh, small, smp,
-        ld, lu, rd0, ru0, ls_d, ls_u, rx_d, rx_u, part_large, lg,
+        bg, bh, gdn, gup, back, sh, small, dsum,
+        ld, lu, rd0, ru0, ls_d, ls_u, rx_d, rx_u, s2, rx2, fin, lg,
         stx, srx, s2x, sfin, sen, hl, hr, cells,
-        send_g, recv_g, send_h, recv_h, send_s, recv_s, load_sem, store_sem,
-    ) = rest[16:]
+        send_g, recv_g, send_h, recv_h, send_s, recv_s, load_sem,
+    ) = rest[9:]
     lon = lax.axis_index("lon")
     dp = lax.axis_index("dp")
     x_hi, y, z = lon // 32, (lon // 8) % 4, lon % 8
@@ -75,10 +75,15 @@
     idx_p = (x_hi * 4 + y) * 4 + dp
     idx_m = (x_lo * 4 + y) * 2 + x_hi
     idx_h = x_hi * 4 + y
+    idx_e = x_hi * 4 + dp
 
     def peer_p(k):
         j = (idx_p + k) % 32
         return j, ((j // 4) * 8 + z, j % 4)
+
+    def peer_e(k):
+        j = (idx_e + k) % 8
+        return j, ((j // 4) * 32 + y * 8 + z, j % 4)
 
     def peer_z(k):
         j = (z + k) % 8
@@ -98,11 +103,6 @@
     ]
     for copy in loads:
         copy.start()
-    stores = [
-        pltpu.make_async_copy(src, dst, store_sem.at[n])
-        for n, (src, dst) in enumerate(zip(made, outputs))
-    ]
-
     barrier = pltpu.get_barrier_semaphore()
     for target in (right, left):
         pl.semaphore_signal(barrier, inc=1, device_id=target, device_id_type=MESH)
@@ -126,7 +126,7 @@
     wp[0:50, 256 + FP : 256 + FP + V] = head[...].astype(F32)
     wd[...] = jnp.zeros(wd.shape, F32)
     wd[0:C, 0:C] = down[...].astype(F32)
-    ga[dp] = wp[:, 0:256].astype(BF16)
+    ga[dp] = (wp[:, 0:128] + pltpu.roll(wp[:, 128:256], V, 1)).astype(BF16)
     gb[dp] = wp[:, 256 : 256 + FP + 128].astype(BF16)
     gd[dp] = wd[...].astype(BF16)
 
@@ -189,9 +189,7 @@
     large_weights[0][0].start()
     large_weights[0][1].start()
     large_weights[1][1].start()
-    first = dot(from_padded, ga[...].reshape(CP, 256))
-    stem_w[...] = first[:, 0:128].astype(BF16)
-    stem_t[...] = first[:, 0:128].T.astype(BF16)
+    stem_w[...] = dot(from_padded, ga[...].reshape(CP, 128)).astype(BF16)
     def stem_pair(s):
         out = dot(stem_w[:, 0:VP], fm[:, s * LAT : (s + 2) * LAT])[0:C].astype(BF16).astype(F32)
         xs[s] = out[:, 0:LAT]
@@ -199,11 +197,11 @@
 
     for s in range(HALO, HALO + COLS, 2):
         stem_pair(s)
-    kern_w = first[0:C, 128:256].astype(BF16)
+    kern_w = stem_w[0:208, :]
     tap_row = lax.broadcasted_iota(jnp.int32, (LAT, 2 * LAT), 0)
     second_half = (lax.broadcasted_iota(jnp.int32, (LAT, 2 * LAT), 1) >= LAT).astype(jnp.int32)
     for t in range(0, SIDE * SIDE, 2):
-        spread = dot(kern_w, jnp.where(tap_row == t + second_half, 1.0, 0.0).astype(BF16))
+        spread = dot(kern_w, jnp.where(tap_row == V + t + second_half, 1.0, 0.0).astype(BF16))[0:C]
         taps[t] = spread[:, 0:LAT]
         if t + 1 < SIDE * SIDE:
             taps[t + 1] = spread[:, LAT : 2 * LAT]
@@ -214,6 +212,7 @@
     for s in list(range(0, HALO, 2)) + list(range(HALO + COLS, SLOTS, 2)):
         stem_pair(s)
 
+    large_weights[1][0].start()
     def conv_forward(block, carry):
         here = pl.ds(pl.multiple_of(block * 8, 8), 8)
         for first_col in (0, 4):
@@ -235,9 +234,9 @@
 
     lax.fori_loop(0, 13, conv_forward, 0)
     pass_on(0)
-    large_weights[1][0].start()
     lax.fori_loop(13, C // 8, conv_forward, 0)
 
+    pass_on(1)
     nh[...] = jnp.zeros(nh.shape, BF16)
     rstds = []
     for i in range(COLS):
@@ -271,7 +270,6 @@
             slope[f : f + FB, part] = half + value * (1.0 - half) * (
                 2.0 * GELU_K + (6.0 * GELU_K * 0.044715) * u2
             )
-    pass_on(1)
     for j in range(2, 4):
         part = pl.ds(j * 2 * LAT, 2 * LAT)
         for f in range(0, FF, FB):
@@ -312,9 +310,23 @@
     sa[idx_p] = jnp.where(lanes == V, ocean_local, mine)
     stage(0, 32, peer_p, lambda j: sa.at[idx_p], sa.at[idx_p])
 
+    gdn[...] = jnp.zeros(gdn.shape, F32)
+    own_down = dot_nt(act[...], mis[...])
+    for d in range(4):
+        gdn[CP * d : CP * d + C, 0:VP] = own_down[C * d : C * d + C]
+    own_head = dot_nt(bo[...], mis[...]).astype(BF16)
+    own_head = dot(to_padded, own_head)
+    for d in range(4):
+        gdn[CP * d + C : CP * d + C + 56, 0:VP] = own_head[64 * d : 64 * d + 56]
+    for d in range(4):
+        for r in range(8):
+            piece = (d % 2) * 16 + (d // 2) * 8 + r
+            ld[piece] = gdn[CP * d + 32 * r : CP * d + 32 * r + 32, :].astype(BF16)
+    away = pl.ds((1 - core) * 16, 16)
+    copy_d = remote(ld.at[away], rd0, send_s.at[2], recv_s.at[2], sibling)
+    copy_d.start()
     nhp[...] = dot(to_padded, nh[...]).astype(BF16)
-    small[:, 128:256] = jnp.zeros((CP, 128), F32)
-    small[:, 128 : 128 + VP] = dot_nt(bo[...], mis[...])
+    stem_t[...] = stem_w[...].astype(F32).T.astype(BF16)
 
     stage_wait(0, 32, sa)
     total = sa[0]
@@ -322,6 +334,10 @@
         total = total + sa[j]
     sb[z] = total
     stage(1, 8, peer_z, lambda j: sb.at[z], sb.at[z])
+    copy_d.wait_recv()
+    for j in range(16):
+        ls_d[j] = (ld[core * 16 + j].astype(F32) + rd0[j].astype(F32)).astype(BF16)
+    stage(4, 16, peer_m, lambda j: ls_d.at[j], rx_d.at[idx_m])
     stage_wait(1, 8, sb)
     total = sb[0]
     for j in range(1, 8):
@@ -332,29 +348,15 @@
     mean_error = jnp.where(valid, total, 0.0) / ocean_count
     ratio = 1.0 + mean_error / threshold
     o_loss[...] = jnp.sum(jnp.where(valid, threshold * jnp.log(ratio), 0.0), axis=1, keepdims=True)
-    stores[5].start()
     factor = jnp.where(valid, 2.0 / (ocean_count * ratio), 0.0)
 
-    small[:, 128:256] = small[:, 128:256] * factor
-    scaled = (head_w[...] * factor).astype(BF16)
+    head_s[...] = (head_w[...] * factor).astype(BF16)
+    scaled = head_s[...]
     for j in range(COLS // 2):
         part = pl.ds(j * 2 * LAT, 2 * LAT)
         grad = dot(scaled[:, 0:VP], mis[:, part])
         bg[:, part] = grad[0:C]
         bh[:, part] = grad.astype(BF16)
-    gdn[FF : FF + 64, :] = jnp.zeros((64, CP), F32)
-    for f in range(0, FF, FB):
-        gdn[f : f + FB, :] = dot_nt(act[f : f + FB, :], bh[...])
-    for d in range(4):
-        for s in range(4):
-            piece = (d % 2) * 16 + (d // 2) * 8 + s * 2
-            block = gdn[C * d + 64 * s : C * d + 64 * s + 64, :]
-            ld[piece] = block[:, 0:128].astype(BF16)
-            ld[piece + 1] = block[:, 128:256].astype(BF16)
-    away = pl.ds((1 - core) * 16, 16)
-    copy_d = remote(ld.at[away], rd0, send_s.at[2], recv_s.at[2], sibling)
-    copy_d.start()
-
     pre[FF:FP, :] = jnp.zeros((FP - FF, CELLS), BF16)
     for j in range(COLS // 2):
         part = pl.ds(j * 2 * LAT, 2 * LAT)
@@ -385,10 +387,6 @@
             mean_gn = jnp.mean(g * normed, axis=0, keepdims=True)
             ms[i] = (rstds[i] * (g - mean_g - normed * mean_gn)).astype(BF16).astype(F32)
 
-    copy_d.wait_recv()
-    for j in range(16):
-        ls_d[j] = (ld[core * 16 + j].astype(F32) + rd0[j].astype(F32)).astype(BF16)
-    stage(4, 16, peer_m, lambda j: ls_d.at[j], rx_d.at[idx_m])
     def conv_backward(block, carry):
         here = pl.ds(pl.multiple_of(block * 8, 8), 8)
         x = [xs[s, here, :] for s in range(SLOTS)]
@@ -421,19 +419,6 @@
         ls_u[j] = (lu[core * 16 + j].astype(F32) + ru0[j].astype(F32)).astype(BF16)
     stage(11, 16, peer_m, lambda j: ls_u.at[j], rx_u.at[idx_m])
     lax.fori_loop(3, C // 8, conv_backward, 0)
-    stage_wait(4, 16, rx_d)
-    rx_d[idx_m] = ls_d[idx_m]
-    large = rx_d[0].astype(F32)
-    for j in range(1, 16):
-        large = large + rx_d[j].astype(F32)
-    part_large[z, 0:64] = large.astype(BF16)
-    stage_wait(11, 16, rx_u)
-    rx_u[idx_m] = ls_u[idx_m]
-    large = rx_u[0].astype(F32)
-    for j in range(1, 16):
-        large = large + rx_u[j].astype(F32)
-    part_large[z, 64:128] = large.astype(BF16)
-    stage(5, 8, peer_z, lambda j: part_large.at[z], part_large.at[z])
     tap_col = lax.broadcasted_iota(jnp.int32, (2 * LAT, LAT), 1)
     lower_half = (lax.broadcasted_iota(jnp.int32, (2 * LAT, LAT), 0) >= LAT).astype(jnp.int32)
     kern = None
@@ -446,23 +431,35 @@
             place = place[0:LAT]
         part_sum = dot(terms, place)
         kern = part_sum if kern is None else kern + part_sum
-    small[0:C, 128:256] = small[0:C, 128:256] + kern
-
+
+    stage_wait(11, 16, rx_u)
+    rx_u[idx_m] = ls_u[idx_m]
+    large = rx_u[0].astype(F32)
+    for j in range(1, 16):
+        large = large + rx_u[j].astype(F32)
+    s2[0:4] = large.astype(BF16).reshape(4, 16, 128)
+    stage_wait(4, 16, rx_d)
+    rx_d[idx_m] = ls_d[idx_m]
+    large = rx_d[0].astype(F32)
+    for j in range(1, 16):
+        large = large + rx_d[j].astype(F32)
+    s2[4:6] = large.astype(BF16).reshape(2, 16, 128)
+    s2[6:8] = jnp.zeros((2, 16, 128), BF16)
+    stage(5, 8, peer_z, lambda j: s2.at[j], rx2.at[z])
     sh[C:CP, :] = jnp.zeros((CP - C, SLOTS * LAT), BF16)
     for s in range(SLOTS):
         value = back[s]
         if HALO <= s < HALO + COLS:
             value = value + bg[:, (s - HALO) * LAT : (s - HALO + 1) * LAT]
         sh[0:C, s * LAT : (s + 1) * LAT] = value.astype(BF16)
-    small[:, 0:128] = jnp.zeros((CP, 128), F32)
+    small[...] = jnp.zeros(small.shape, F32)
     small[:, 0:VP] = dot_nt(sh[...], fm[...])
-    smp[...] = dot(to_padded, small[...].astype(BF16)).astype(BF16)
-    for d in range(4):
-        for s in range(4):
-            at = 64 * d + 16 * s
-            stx[s * 4 + d] = smp[at : at + 16, 0:128]
-            stx[16 + s * 4 + d] = smp[at : at + 16, 128:256]
-    stage(6, 32, peer_p, lambda j: stx.at[j], srx.at[idx_p])
+    small[0:C, :] = small[0:C, :] + kern
+    tiny = dot(to_padded, small[...].astype(BF16))
+    for j in range(8):
+        at = 64 * (j % 4) + 32 * (j // 4)
+        stx[j] = tiny[at : at + 32].astype(BF16)
+    stage(6, 8, peer_e, lambda j: stx.at[j], srx.at[idx_e])
 
     for s in list(range(0, HALO, 2)) + list(range(HALO + COLS, SLOTS, 2)):
         value = dot(stem_t[0:VP, :], sh[:, s * LAT : (s + 2) * LAT]).astype(BF16)
@@ -479,19 +476,23 @@
         cells[2 * j] = value[:, 0:LAT]
         cells[2 * j + 1] = value[:, LAT : 2 * LAT]
 
-    stage_wait(6, 32, srx)
-    srx[idx_p] = stx[idx_p]
+    stage_wait(5, 8, rx2)
+    rx2[z] = s2[z]
+    part_sum = rx2[0].astype(F32)
+    for j in range(1, 8):
+        part_sum = part_sum + rx2[j].astype(F32)
+    fin[z] = part_sum.astype(BF16)
+    stage(7, 8, peer_z, lambda j: fin.at[z], fin.at[z])
+    stage_wait(6, 8, srx)
+    srx[idx_e] = stx[idx_e]
     tiny = srx[0].astype(F32)
-    for j in range(1, 32):
+    for j in range(1, 8):
         tiny = tiny + srx[j].astype(F32)
     s2x[z] = tiny.astype(BF16)
     stage(8, 8, peer_z, lambda j: s2x.at[z], s2x.at[z])
 
-    stage_wait(5, 8, part_large)
-    large = part_large[0].astype(F32)
-    for j in range(1, 8):
-        large = large + part_large[j].astype(F32)
-    lg[idx_h] = large.astype(BF16)
+    stage_wait(7, 8, fin)
+    lg[idx_h] = fin[0:6].reshape(96, 128)
     stage(9, 8, peer_h, lambda j: lg.at[idx_h], lg.at[idx_h])
 
     stage_wait(8, 8, s2x)
@@ -510,48 +511,37 @@
         if i < 6:
             value = value + hl[i].astype(F32)
         o_sens[pl.ds(i, V, stride=COLS), :] = (value * ocean_count)[0:V]
-    stores[6].start()
 
     stage_wait(9, 8, lg)
     for s in range(4):
         rows = 16 if s < 3 else 2
         for l in range(7):
             width = min(128, FF - 128 * l)
-            at = 64 + 16 * (l % 4)
+            at = 16 * (l % 4)
             piece = lg[s + 4 * (l // 4), at : at + 16, :].astype(F32)
             o_up[16 * s : 16 * s + rows, 128 * l : 128 * l + width] = piece[0:rows, 0:width]
-        rows = 64 if s < 3 else 8
-        o_down[64 * s : 64 * s + rows, 0:128] = lg[s, 0:64, :].astype(F32)[0:rows]
-        o_down[64 * s : 64 * s + rows, 128:C] = lg[s + 4, 0:64, :].astype(F32)[0:rows, 0 : C - 128]
-    stores[2].start()
-    stores[3].start()
+    for r in range(8):
+        dsum[32 * r : 32 * r + 32, :] = lg[(r % 2) * 4 + r // 2, 64:96, :]
+    o_down[...] = dot_nt(dsum[...], head_s[...])[0:C, 0:C]
+    o_head[...] = (dsum[...].astype(F32)[C : C + 50] * factor)[:, 0:V]
     stage_wait(10, 8, sfin)
-    for s in range(4):
-        rows = 16 if s < 3 else 2
-        o_stem[16 * s : 16 * s + rows, :] = sfin[s].astype(F32)[0:rows, 0:V]
-        piece = sfin[4 + s].astype(F32)
-        o_head[16 * s : 16 * s + rows, :] = piece[0:rows, 0:V]
-        o_kern[16 * s : 16 * s + rows, :] = pltpu.roll(piece, LAT - V, 1)[0:rows, 0:49]
-    for n in (0, 1, 4):
-        stores[n].start()
+    for h, rows in ((0, 32), (1, 18)):
+        tiny = sfin[4 * h].astype(F32)
+        for j in range(1, 4):
+            tiny = tiny + sfin[4 * h + j].astype(F32)
+        o_stem[32 * h : 32 * h + rows, :] = tiny[0:rows, 0:V]
+        o_kern[32 * h : 32 * h + rows, :] = pltpu.roll(tiny, LAT - V, 1)[0:rows, 0:49]
     for copy in first_weights + halo + list(large_weights[0] + large_weights[1]):
         copy.wait_send()
     for copy in [copy_d, copy_u, copy_l, copy_r] + pending:
         copy.wait_send()
-    for copy in stores:
-        copy.wait()
 
 
 def hand_over(*refs):
-    ins, outs, held, sems = refs[:7], refs[7:14], refs[14:21], refs[21]
-    into = [pltpu.make_async_copy(ins[n], held[n], sems.at[n]) for n in range(7)]
-    away = [pltpu.make_async_copy(held[n], outs[n], sems.at[7 + n]) for n in range(7)]
-    for copy in into:
+    copies = [pltpu.make_async_copy(refs[n], refs[7 + n], refs[14].at[n]) for n in range(7)]
+    for copy in copies:
         copy.start()
-    for n in range(7):
-        into[n].wait()
-        away[n].start()
-    for copy in away:
+    for copy in copies:
         copy.wait()
 
 
@@ -565,20 +555,13 @@
     ((50, FF), BF16),
     ((C, C), BF16),
     ((50, V), BF16),
-    ((50, V), F32),
-    ((50, SIDE * SIDE), F32),
-    ((50, FF), F32),
-    ((C, C), F32),
-    ((50, V), F32),
-    ((1, 1), F32),
-    ((V * COLS, LAT), F32),
     ((VP * COLS, LAT), F32),
     ((VP * COLS, LAT), F32),
     ((SLOTS, VP, LAT), BF16),
     ((VP, SLOTS * LAT), BF16),
     ((64, 256 + FP + 128), F32),
     ((208, CP), F32),
-    ((4, 64, 256), BF16),
+    ((4, 64, 128), BF16),
     ((4, 64, FP + 128), BF16),
     ((4, 208, CP), BF16),
     ((CP, 128), BF16),
@@ -586,6 +569,7 @@
     ((CP, FP), BF16),
     ((FP, CP), BF16),
     ((CP, 128), F32),
+    ((CP, 128), BF16),
     ((128, CP), BF16),
     ((FF, CP), BF16),
     ((CP, FF), BF16),
@@ -607,26 +591,28 @@
     ((8, 1, LAT), F32),
     ((C, CELLS), F32),
     ((CP, CELLS), BF16),
-    ((FF + 64, CP), F32),
+    ((4 * CP, 128), F32),
     ((CP, FP), F32),
     ((SLOTS, C, LAT), F32),
     ((CP, SLOTS * LAT), BF16),
-    ((CP, 256), F32),
-    ((CP, 256), BF16),
+    ((CP, 128), F32),
+    ((CP, 128), BF16),
+    ((32, 32, 128), BF16),
     ((32, 64, 128), BF16),
-    ((32, 64, 128), BF16),
+    ((16, 32, 128), BF16),
     ((16, 64, 128), BF16),
+    ((16, 32, 128), BF16),
     ((16, 64, 128), BF16),
+    ((16, 32, 128), BF16),
     ((16, 64, 128), BF16),
-    ((16, 64, 128), BF16),
-    ((16, 64, 128), BF16),
-    ((16, 64, 128), BF16),
-    ((8, 128, 128), BF16),
-    ((8, 128, 128), BF16),
-    ((32, 16, 128), BF16),
-    ((32, 16, 128), BF16),
     ((8, 16, 128), BF16),
     ((8, 16, 128), BF16),
+    ((8, 16, 128), BF16),
+    ((8, 96, 128), BF16),
+    ((8, 32, 128), BF16),
+    ((8, 32, 128), BF16),
+    ((8, 32, 128), BF16),
+    ((8, 32, 128), BF16),
     ((12, VP, LAT), BF16),
     ((6, VP, LAT), BF16),
     ((6, VP, LAT), BF16),
@@ -638,16 +624,17 @@
     fields, targets, land_sea, clip_level, stem_weight, dw_kernel, up_weight, down_weight, head_weight
 ):
     anywhere = pl.BlockSpec(memory_space=pl.ANY)
+    vmem = pl.BlockSpec(memory_space=pltpu.VMEM)
     dma = pltpu.SemaphoreType.DMA
     shapes = [(50, V), (50, 49), (50, FF), (C, C), (50, V), (1, 1), (V * COLS, LAT)]
     results = [jax.ShapeDtypeStruct(s, F32) for s in shapes]
     made = pl.pallas_call(
         body,
-        out_shape=results,
+        out_shape=[pltpu.VMEM(s, F32) for s in shapes],
         in_specs=[anywhere] * 9,
-        out_specs=[anywhere] * 7,
+        out_specs=[vmem] * 7,
         scratch_shapes=[pltpu.VMEM(s, t) for s, t in SCRATCH]
-        + [dma((n,)) for n in (9, 9, 4, 4, 12, 12, 9, 7)],
+        + [dma((n,)) for n in (9, 9, 4, 4, 12, 12, 9)],
         compiler_params=pltpu.CompilerParams(
             collective_id=0, has_side_effects=True, vmem_limit_bytes=58 * 1024 * 1024
         ),
@@ -665,10 +652,10 @@
     outs = pl.pallas_call(
         hand_over,
         out_shape=results,
-        in_specs=[anywhere] * 7,
+        in_specs=[vmem] * 7,
         out_specs=[anywhere] * 7,
-        scratch_shapes=[pltpu.VMEM(s, F32) for s in shapes] + [dma((14,))],
-    )(*made)
+        scratch_shapes=[dma((7,))],
+    )(*[pltpu.with_memory_space_constraint(m, pltpu.VMEM) for m in made])
     return (
         outs[0], outs[1], outs[2], outs[3], outs[4],
         outs[5].reshape(()),

time: 69.2 us -> 62.4 us (0.902)
  Pallas kernels: 67.2 us -> 61.2 us
    pallas_call x2, Pallas kernels: 67.2 us -> 61.2 us  [the longest x1 59.7 us: shards(): pl.pallas_call(body, out_shape=[pltpu.VMEM(s, F32) for s in shapes], in_s...]
where the time goes in v1:
time: 62.4 us; the launch traced here: 61.9 us
  Pallas kernels  61.2 us (98%)
  between operations  0.64 us (1%)
    pallas_call x1, Pallas kernels, shards(): pl.pallas_call(body, out_shape=[pltpu.VMEM(s, F32) for s in shapes], in_s...  59.7 us
    pallas_call x1, Pallas kernels, shards(): pl.pallas_call(hand_over, out_shape=results, in_specs=[vmem] * 7, out_spe...  1.58 us

profile of v1, /device:TPU:6, one launch (start us, length us, event | category | flops | bytes accessed | tf_op | source)
XLA Modules:
  0.0 61.9 jit_solution(11204277976113850922)
XLA Ops:
  0.6 59.7 %shard_map.144 = (f32[50,77]{1,0:T(8,128)S(1)}, f32[50,49]{1,0:T(8,128)S(1)}, f32[50,800]{1,0:T(8,128)S(1)}, f32[200,200]{1,0:T(8,128)S(1)}, f32[50,77]{1,0:T(8,...) custom-call(bf16[77,8,128]{2,1,0:T(8,128)(2,1)} %bitcast.5, bf16[77,8,128]{2,1,0:T(8,128)(2,1)} %bitcast.6, ...), custom_call_target="tpu_custom_call" | custom-call | tf_op jit(solution)/shard_map/pallas_call | solution.py:631
  60.3 1.6 %shard_map.145 = (f32[50,77]{1,0:T(8,128)}, f32[50,49]{1,0:T(8,128)}, f32[50,800]{1,0:T(8,128)}, f32[200,200]{1,0:T(8,128)}, f32[50,77]{1,0:T(8,128)}, /*index=5*/f32[1,1]{1,0:T(1,128)}, f32[616,128]{1,0:T(8,128)}) custom-call(f32[50,77]{1,0:T(8,128)S(1)} %get-tuple-element.21.refs_0_, f32[50,49]{1,0:T(8,128)S(1)} %get-tuple-element.22.refs_1_, ...), custom_call_target="tpu_custom_call" | custom-call | tf_op jit(solution)/shard_map/pallas_call | solution.py:652

commit v2 on v1

--- a/solution.py
+++ b/solution.py
@@ -1,3 +1,5 @@
+import itertools
+
 import jax
 import jax.numpy as jnp
 from jax import lax
@@ -15,7 +17,7 @@
 CP = 256
 FF = 800
 FP = 896
-FB = 160
+FB = 400
 COLS = 8
 LAT = 128
 SIDE = 7
@@ -44,6 +46,17 @@
     )
 
 
+def hops(offset):
+    a, b, c, d, e = offset
+    x = {(0, 0): 0, (0, 1): 1, (1, 0): 2, (1, 1): 1}[a, d]
+    return x + min(b, 4 - b) + min(c, 8 - c) + 0.5 * e
+
+
+def group(*sizes):
+    offsets = itertools.product(*(range(n) for n in sizes))
+    return sorted((o for o in offsets if any(o)), key=lambda o: -hops(o))
+
+
 def padded_row(channel):
     step = (channel >= 50).astype(jnp.int32)
     step += (channel >= 100).astype(jnp.int32)
@@ -59,9 +72,9 @@
     (
     f32a, f32b, fbuf, fm, wp, wd, ga, gb, gd,
         stem_w, stem_t, up_w, up_t, head_w, head_s, head_t, down_w, down_t, down_f,
-        taps, corrs, xs, ms, nh, nhp, act, slope, pre, bo, mis, limits, sq, sa, sb,
-        bg, bh, gdn, gup, back, sh, small, dsum,
-        ld, lu, rd0, ru0, ls_d, ls_u, rx_d, rx_u, s2, rx2, fin, lg,
+        taps, partial, corrs, xs, ms, nh, act, slope, pre, bo, mis, limits, sq, sa, sb,
+        bg, bh, gdn, gup, flat, back, sh, small, dsum,
+        ld, lu, rd0, ru0, ls_d, ls_u, rx_d, rx_u, part_u, lg_u, part_d, lg_d,
         stx, srx, s2x, sfin, sen, hl, hr, cells,
         send_g, recv_g, send_h, recv_h, send_s, recv_s, load_sem,
     ) = rest[9:]
@@ -77,25 +90,23 @@
     idx_h = x_hi * 4 + y
     idx_e = x_hi * 4 + dp
 
-    def peer_p(k):
-        j = (idx_p + k) % 32
-        return j, ((j // 4) * 8 + z, j % 4)
-
-    def peer_e(k):
-        j = (idx_e + k) % 8
-        return j, ((j // 4) * 32 + y * 8 + z, j % 4)
-
-    def peer_z(k):
-        j = (z + k) % 8
-        return j, (x_hi * 32 + y * 8 + j, dp)
-
-    def peer_m(k):
-        j = (idx_m + k) % 16
-        return j, ((j % 2) * 32 + ((j // 2) % 4) * 8 + z, (j // 8) * 2 + core)
-
-    def peer_h(k):
-        j = (idx_h + k) % 8
-        return j, (j * 8 + z, dp)
+    busy = ((y == 3) & (z == 0)) | ((y == 0) & (z == 7))
+    helper = ((y == 2) & (z == 0)) | ((y == 1) & (z == 7))
+    alone, plain = jnp.logical_not(busy), jnp.logical_not(busy | helper)
+    helped = (x_hi * 32 + ((y + jnp.where(z == 0, 1, 3)) % 4) * 8 + z, dp)
+
+    def peer(offset):
+        a, b, c, d, e = offset
+        return (x_hi + a) % 2, (y + b) % 4, (z + c) % 8, (x_lo + d) % 2, (core + e) % 2
+
+    def device(at):
+        return at[0] * 32 + at[1] * 8 + at[2], at[3] * 2 + at[4]
+
+    PLANE = group(2, 4, 1, 2, 2), lambda at: (at[0] * 4 + at[1]) * 4 + at[3] * 2 + at[4]
+    RING = group(1, 1, 8, 1, 1), lambda at: at[2]
+    CORES = group(2, 4, 1, 2, 1), lambda at: (at[3] * 4 + at[1]) * 2 + at[0]
+    SHARE = group(2, 4, 1, 1, 1), lambda at: at[0] * 4 + at[1]
+    ROW = group(2, 1, 1, 2, 2), lambda at: at[0] * 4 + at[3] * 2 + at[4]
 
     loads = [
         pltpu.make_async_copy(src, dst, load_sem.at[n])
@@ -104,12 +115,16 @@
     for copy in loads:
         copy.start()
     barrier = pltpu.get_barrier_semaphore()
+    for offset in RING[0]:
+        pl.semaphore_signal(
+            barrier, inc=1, device_id=device(peer(offset)), device_id_type=MESH
+        )
     for target in (right, left):
         pl.semaphore_signal(barrier, inc=1, device_id=target, device_id_type=MESH)
-    for k in range(1, 32):
-        pl.semaphore_signal(barrier, inc=1, device_id=peer_p(k)[1], device_id_type=MESH)
-    for k in range(1, 8):
-        pl.semaphore_signal(barrier, inc=1, device_id=peer_z(k)[1], device_id_type=MESH)
+    for offset in PLANE[0]:
+        pl.semaphore_signal(
+            barrier, inc=1, device_id=device(peer(offset)), device_id_type=MESH
+        )
 
     for copy in loads:
         copy.wait()
@@ -155,16 +170,31 @@
             )
         )
 
+    for copy in halo:
+        copy.start()
+    pl.when(alone)(large_weights[0][0].start)
+
+    help_copies = [
+        remote(buf.at[far], buf.at[far], send_g.at[9 + a], recv_g.at[3 + 3 * a], helped)
+        for a, buf in enumerate((gb, gd))
+    ]
+
     def pass_on(a):
         large_weights[a][0].wait_recv()
         large_weights[a][2].start()
 
+    def help_on(a):
+        pass_on(a)
+        help_copies[a].start()
+
     pending = []
 
     def stage(index, count, peers, src, dst):
-        for k in range(1, count):
-            j, device = peers(k)
-            remote(src(j), dst, send_s.at[index], recv_s.at[index], device).start()
+        for offset in peers[0][: count - 1]:
+            at = peer(offset)
+            remote(
+                src(peers[1](at)), dst, send_s.at[index], recv_s.at[index], device(at)
+            ).start()
 
     def stage_wait(index, count, buf):
         whole = buf.at[pl.ds(0, count - 1)]
@@ -182,13 +212,9 @@
     for i in range(COLS):
         fm[:, (HALO + i) * LAT : (HALO + i + 1) * LAT] = fbuf[HALO + i]
 
-    for copy in halo:
-        copy.start()
     for copy in first_weights:
         copy.wait_recv()
-    large_weights[0][0].start()
     large_weights[0][1].start()
-    large_weights[1][1].start()
     stem_w[...] = dot(from_padded, ga[...].reshape(CP, 128)).astype(BF16)
     def stem_pair(s):
         out = dot(stem_w[:, 0:VP], fm[:, s * LAT : (s + 2) * LAT])[0:C].astype(BF16).astype(F32)
@@ -205,6 +231,27 @@
         taps[t] = spread[:, 0:LAT]
         if t + 1 < SIDE * SIDE:
             taps[t + 1] = spread[:, LAT : 2 * LAT]
+    def own_taps(i):
+        return [p for p in range(SIDE) if HALO <= i + 2 * p < HALO + COLS]
+
+    def conv_own(block, carry):
+        here = pl.ds(pl.multiple_of(block * 8, 8), 8)
+        x = {s: xs[s, here, :] for s in range(HALO, HALO + COLS)}
+        for q in range(SIDE):
+            w = [taps[p * SIDE + q, here, :] for p in range(SIDE)]
+            for i in range(COLS):
+                total = None
+                for p in own_taps(i):
+                    term = w[p] * x[i + 2 * p]
+                    total = term if total is None else total + term
+                partial[q * COLS + i, here, :] = total
+        return carry
+
+    pl.when(alone)(large_weights[1][0].start)
+    large_weights[1][1].start()
+    pl.when(helper)(lambda: help_on(0))
+    lax.fori_loop(0, C // 8, conv_own, 0)
+    pl.when(plain)(lambda: pass_on(0))
     for copy in halo:
         copy.wait_recv()
     for s in list(range(0, HALO)) + list(range(HALO + COLS, SLOTS)):
@@ -212,31 +259,30 @@
     for s in list(range(0, HALO, 2)) + list(range(HALO + COLS, SLOTS, 2)):
         stem_pair(s)
 
-    large_weights[1][0].start()
     def conv_forward(block, carry):
         here = pl.ds(pl.multiple_of(block * 8, 8), 8)
-        for first_col in (0, 4):
-            x = [xs[first_col + s, here, :] for s in range(4 + 2 * HALO)]
-            out = [None] * 4
-            for q in range(SIDE):
-                b = (q - 3) * 2
-                w = [taps[p * SIDE + q, here, :] for p in range(SIDE)]
-                for i in range(4):
-                    total = w[0] * x[i]
-                    for p in range(1, SIDE):
+        x = {s: xs[s, here, :] for s in range(SLOTS) if not HALO <= s < HALO + COLS}
+        out = [None] * COLS
+        for q in range(SIDE):
+            b = (q - 3) * 2
+            w = [taps[p * SIDE + q, here, :] for p in range(SIDE)]
+            for i in range(COLS):
+                total = partial[q * COLS + i, here, :]
+                for p in range(SIDE):
+                    if p not in own_taps(i):
                         total = total + w[p] * x[i + 2 * p]
-                    if b != 0:
-                        total = jnp.where(keep[b], pltpu.roll(total, (-b) % LAT, 1), 0.0)
-                    out[i] = total if out[i] is None else out[i] + total
-            for i in range(4):
-                ms[first_col + i, here, :] = out[i]
+                if b != 0:
+                    total = jnp.where(keep[b], pltpu.roll(total, (-b) % LAT, 1), 0.0)
+                out[i] = total if out[i] is None else out[i] + total
+        for i in range(COLS):
+            ms[i, here, :] = out[i]
         return carry
 
     lax.fori_loop(0, 13, conv_forward, 0)
-    pass_on(0)
+    pl.when(helper)(lambda: help_on(1))
+    pl.when(busy)(lambda: pass_on(0))
     lax.fori_loop(13, C // 8, conv_forward, 0)
 
-    pass_on(1)
     nh[...] = jnp.zeros(nh.shape, BF16)
     rstds = []
     for i in range(COLS):
@@ -255,6 +301,7 @@
     up_t[...] = second[:, 0:FP].T.astype(BF16)
     head_w[...] = second[:, FP : FP + 128]
     head_t[...] = second[:, FP : FP + 128].T.astype(BF16)
+    pl.when(plain)(lambda: pass_on(1))
     limits[...] = jnp.ones((1, LAT), F32)
     limits[:, 0:V] = clip[...].astype(F32) / 16.0
     sq[...] = jnp.zeros(sq.shape, F32)
@@ -270,6 +317,7 @@
             slope[f : f + FB, part] = half + value * (1.0 - half) * (
                 2.0 * GELU_K + (6.0 * GELU_K * 0.044715) * u2
             )
+    pl.when(busy)(lambda: pass_on(1))
     for j in range(2, 4):
         part = pl.ds(j * 2 * LAT, 2 * LAT)
         for f in range(0, FF, FB):
@@ -308,7 +356,7 @@
     ocean_local = jnp.sum(land[...].astype(F32))
     mine = jnp.sum(sq[...].T, axis=0, keepdims=True)
     sa[idx_p] = jnp.where(lanes == V, ocean_local, mine)
-    stage(0, 32, peer_p, lambda j: sa.at[idx_p], sa.at[idx_p])
+    stage(0, 32, PLANE, lambda j: sa.at[idx_p], sa.at[idx_p])
 
     gdn[...] = jnp.zeros(gdn.shape, F32)
     own_down = dot_nt(act[...], mis[...])
@@ -325,7 +373,7 @@
     away = pl.ds((1 - core) * 16, 16)
     copy_d = remote(ld.at[away], rd0, send_s.at[2], recv_s.at[2], sibling)
     copy_d.start()
-    nhp[...] = dot(to_padded, nh[...]).astype(BF16)
+    flat[...] = jnp.zeros(flat.shape, F32)
     stem_t[...] = stem_w[...].astype(F32).T.astype(BF16)
 
     stage_wait(0, 32, sa)
@@ -333,11 +381,11 @@
     for j in range(1, 32):
         total = total + sa[j]
     sb[z] = total
-    stage(1, 8, peer_z, lambda j: sb.at[z], sb.at[z])
+    stage(1, 8, RING, lambda j: sb.at[z], sb.at[z])
     copy_d.wait_recv()
     for j in range(16):
         ls_d[j] = (ld[core * 16 + j].astype(F32) + rd0[j].astype(F32)).astype(BF16)
-    stage(4, 16, peer_m, lambda j: ls_d.at[j], rx_d.at[idx_m])
+    stage(4, 16, CORES, lambda j: ls_d.at[j], rx_d.at[idx_m])
     stage_wait(1, 8, sb)
     total = sb[0]
     for j in range(1, 8):
@@ -364,15 +412,17 @@
             pre[f : f + FB, part] = (
                 dot(down_w[f : f + FB, :], bh[:, part]) * slope[f : f + FB, part]
             ).astype(BF16)
-    gup[...] = dot_nt(nhp[...], pre[...])
+    up_grad = dot_nt(nh[...], pre[...])
+    for l in range(7):
+        gup[l] = up_grad[:, 128 * l : 128 * l + 128]
     for d in range(4):
-        for s in range(4):
-            piece = (d % 2) * 16 + (d // 2) * 8 + s * 2
-            for l in range(7):
-                lu[piece + l // 4, 16 * (l % 4) : 16 * (l % 4) + 16, :] = gup[
-                    64 * d + 16 * s : 64 * d + 16 * s + 16, 128 * l : 128 * l + 128
-                ].astype(BF16)
-            lu[piece + 1, 48:64, :] = jnp.zeros((16, 128), BF16)
+        for l in range(7):
+            at = 384 * d + 50 * l
+            flat[at : at + 50, :] = gup[l, 50 * d : 50 * d + 50, :]
+    for d in range(4):
+        for r in range(8):
+            piece = (d % 2) * 16 + (d // 2) * 8 + r
+            lu[piece] = flat[384 * d + 48 * r : 384 * d + 48 * r + 48, :].astype(BF16)
     copy_u = remote(lu.at[away], ru0, send_s.at[3], recv_s.at[3], sibling)
     copy_u.start()
 
@@ -386,6 +436,14 @@
             mean_g = jnp.mean(g, axis=0, keepdims=True)
             mean_gn = jnp.mean(g * normed, axis=0, keepdims=True)
             ms[i] = (rstds[i] * (g - mean_g - normed * mean_gn)).astype(BF16).astype(F32)
+
+    stage_wait(4, 16, rx_d)
+    rx_d[idx_m] = ls_d[idx_m]
+    large = rx_d[0].astype(F32)
+    for j in range(1, 16):
+        large = large + rx_d[j].astype(F32)
+    part_d[z] = large.astype(BF16)
+    stage(7, 8, RING, lambda j: part_d.at[z], part_d.at[z])
 
     def conv_backward(block, carry):
         here = pl.ds(pl.multiple_of(block * 8, 8), 8)
@@ -417,8 +475,24 @@
     copy_u.wait_recv()
     for j in range(16):
         ls_u[j] = (lu[core * 16 + j].astype(F32) + ru0[j].astype(F32)).astype(BF16)
-    stage(11, 16, peer_m, lambda j: ls_u.at[j], rx_u.at[idx_m])
-    lax.fori_loop(3, C // 8, conv_backward, 0)
+    stage(11, 16, CORES, lambda j: ls_u.at[j], rx_u.at[idx_m])
+    lax.fori_loop(3, 22, conv_backward, 0)
+
+    stage_wait(7, 8, part_d)
+    large = part_d[0].astype(F32)
+    for j in range(1, 8):
+        large = large + part_d[j].astype(F32)
+    lg_d[idx_h] = large.astype(BF16)
+    stage(12, 8, SHARE, lambda j: lg_d.at[idx_h], lg_d.at[idx_h])
+    stage_wait(11, 16, rx_u)
+    rx_u[idx_m] = ls_u[idx_m]
+    large = rx_u[0].astype(F32)
+    for j in range(1, 16):
+        large = large + rx_u[j].astype(F32)
+    part_u[z] = large.astype(BF16)
+    stage(5, 8, RING, lambda j: part_u.at[z], part_u.at[z])
+
+    lax.fori_loop(22, C // 8, conv_backward, 0)
     tap_col = lax.broadcasted_iota(jnp.int32, (2 * LAT, LAT), 1)
     lower_half = (lax.broadcasted_iota(jnp.int32, (2 * LAT, LAT), 0) >= LAT).astype(jnp.int32)
     kern = None
@@ -432,20 +506,6 @@
         part_sum = dot(terms, place)
         kern = part_sum if kern is None else kern + part_sum
 
-    stage_wait(11, 16, rx_u)
-    rx_u[idx_m] = ls_u[idx_m]
-    large = rx_u[0].astype(F32)
-    for j in range(1, 16):
-        large = large + rx_u[j].astype(F32)
-    s2[0:4] = large.astype(BF16).reshape(4, 16, 128)
-    stage_wait(4, 16, rx_d)
-    rx_d[idx_m] = ls_d[idx_m]
-    large = rx_d[0].astype(F32)
-    for j in range(1, 16):
-        large = large + rx_d[j].astype(F32)
-    s2[4:6] = large.astype(BF16).reshape(2, 16, 128)
-    s2[6:8] = jnp.zeros((2, 16, 128), BF16)
-    stage(5, 8, peer_z, lambda j: s2.at[j], rx2.at[z])
     sh[C:CP, :] = jnp.zeros((CP - C, SLOTS * LAT), BF16)
     for s in range(SLOTS):
         value = back[s]
@@ -459,7 +519,7 @@
     for j in range(8):
         at = 64 * (j % 4) + 32 * (j // 4)
         stx[j] = tiny[at : at + 32].astype(BF16)
-    stage(6, 8, peer_e, lambda j: stx.at[j], srx.at[idx_e])
+    stage(6, 8, ROW, lambda j: stx.at[j], srx.at[idx_e])
 
     for s in list(range(0, HALO, 2)) + list(range(HALO + COLS, SLOTS, 2)):
         value = dot(stem_t[0:VP, :], sh[:, s * LAT : (s + 2) * LAT]).astype(BF16)
@@ -476,31 +536,33 @@
         cells[2 * j] = value[:, 0:LAT]
         cells[2 * j + 1] = value[:, LAT : 2 * LAT]
 
-    stage_wait(5, 8, rx2)
-    rx2[z] = s2[z]
-    part_sum = rx2[0].astype(F32)
-    for j in range(1, 8):
-        part_sum = part_sum + rx2[j].astype(F32)
-    fin[z] = part_sum.astype(BF16)
-    stage(7, 8, peer_z, lambda j: fin.at[z], fin.at[z])
     stage_wait(6, 8, srx)
     srx[idx_e] = stx[idx_e]
     tiny = srx[0].astype(F32)
     for j in range(1, 8):
         tiny = tiny + srx[j].astype(F32)
     s2x[z] = tiny.astype(BF16)
-    stage(8, 8, peer_z, lambda j: s2x.at[z], s2x.at[z])
-
-    stage_wait(7, 8, fin)
-    lg[idx_h] = fin[0:6].reshape(96, 128)
-    stage(9, 8, peer_h, lambda j: lg.at[idx_h], lg.at[idx_h])
+    stage(8, 8, RING, lambda j: s2x.at[z], s2x.at[z])
+
+    stage_wait(5, 8, part_u)
+    large = part_u[0].astype(F32)
+    for j in range(1, 8):
+        large = large + part_u[j].astype(F32)
+    lg_u[idx_h] = large.astype(BF16)
+    stage(9, 8, SHARE, lambda j: lg_u.at[idx_h], lg_u.at[idx_h])
+
+    stage_wait(12, 8, lg_d)
+    for r in range(8):
+        dsum[32 * r : 32 * r + 32, :] = lg_d[(r % 2) * 4 + r // 2]
+    o_down[...] = dot_nt(dsum[...], head_s[...])[0:C, 0:C]
+    o_head[...] = (dsum[...].astype(F32)[C : C + 50] * factor)[:, 0:V]
 
     stage_wait(8, 8, s2x)
     tiny = s2x[0].astype(F32)
     for j in range(1, 8):
         tiny = tiny + s2x[j].astype(F32)
     sfin[idx_h] = tiny.astype(BF16)
-    stage(10, 8, peer_h, lambda j: sfin.at[idx_h], sfin.at[idx_h])
+    stage(10, 8, SHARE, lambda j: sfin.at[idx_h], sfin.at[idx_h])
 
     copy_l.wait_recv()
     copy_r.wait_recv()
@@ -512,18 +574,12 @@
             value = value + hl[i].astype(F32)
         o_sens[pl.ds(i, V, stride=COLS), :] = (value * ocean_count)[0:V]
 
-    stage_wait(9, 8, lg)
-    for s in range(4):
-        rows = 16 if s < 3 else 2
-        for l in range(7):
-            width = min(128, FF - 128 * l)
-            at = 16 * (l % 4)
-            piece = lg[s + 4 * (l // 4), at : at + 16, :].astype(F32)
-            o_up[16 * s : 16 * s + rows, 128 * l : 128 * l + width] = piece[0:rows, 0:width]
+    stage_wait(9, 8, lg_u)
     for r in range(8):
-        dsum[32 * r : 32 * r + 32, :] = lg[(r % 2) * 4 + r // 2, 64:96, :]
-    o_down[...] = dot_nt(dsum[...], head_s[...])[0:C, 0:C]
-    o_head[...] = (dsum[...].astype(F32)[C : C + 50] * factor)[:, 0:V]
+        flat[48 * r : 48 * r + 48, :] = lg_u[(r % 2) * 4 + r // 2].astype(F32)
+    for l in range(7):
+        width = min(128, FF - 128 * l)
+        o_up[:, 128 * l : 128 * l + width] = flat[50 * l : 50 * l + 50, 0:width]
     stage_wait(10, 8, sfin)
     for h, rows in ((0, 32), (1, 18)):
         tiny = sfin[4 * h].astype(F32)
@@ -531,16 +587,27 @@
             tiny = tiny + sfin[4 * h + j].astype(F32)
         o_stem[32 * h : 32 * h + rows, :] = tiny[0:rows, 0:V]
         o_kern[32 * h : 32 * h + rows, :] = pltpu.roll(tiny, LAT - V, 1)[0:rows, 0:49]
-    for copy in first_weights + halo + list(large_weights[0] + large_weights[1]):
+    for copy in first_weights + halo + [large_weights[a][i] for a in (0, 1) for i in (1, 2)]:
         copy.wait_send()
+
+    @pl.when(alone)
+    def _():
+        large_weights[0][0].wait_send()
+        large_weights[1][0].wait_send()
+
+    @pl.when(helper)
+    def _():
+        help_copies[0].wait_send()
+        help_copies[1].wait_send()
+
     for copy in [copy_d, copy_u, copy_l, copy_r] + pending:
         copy.wait_send()
 
 
 def hand_over(*refs):
     copies = [pltpu.make_async_copy(refs[n], refs[7 + n], refs[14].at[n]) for n in range(7)]
-    for copy in copies:
-        copy.start()
+    for n in (6, 2, 3, 0, 1, 4, 5):
+        copies[n].start()
     for copy in copies:
         copy.wait()
 
@@ -575,10 +642,10 @@
     ((CP, FF), BF16),
     ((FF, CP), F32),
     ((SIDE * SIDE, C, LAT), F32),
+    ((SIDE * COLS, C, LAT), F32),
     ((SIDE * SIDE, C, LAT), F32),
     ((SLOTS, C, LAT), F32),
     ((COLS, C, LAT), F32),
-    ((CP, CELLS), BF16),
     ((CP, CELLS), BF16),
     ((FF, CELLS), BF16),
     ((FF, CELLS), F32),
@@ -592,23 +659,24 @@
     ((C, CELLS), F32),
     ((CP, CELLS), BF16),
     ((4 * CP, 128), F32),
-    ((CP, FP), F32),
+    ((7, CP, 128), F32),
+    ((4 * 384, 128), F32),
     ((SLOTS, C, LAT), F32),
     ((CP, SLOTS * LAT), BF16),
     ((CP, 128), F32),
     ((CP, 128), BF16),
     ((32, 32, 128), BF16),
-    ((32, 64, 128), BF16),
+    ((32, 48, 128), BF16),
     ((16, 32, 128), BF16),
-    ((16, 64, 128), BF16),
+    ((16, 48, 128), BF16),
     ((16, 32, 128), BF16),
-    ((16, 64, 128), BF16),
+    ((16, 48, 128), BF16),
     ((16, 32, 128), BF16),
-    ((16, 64, 128), BF16),
-    ((8, 16, 128), BF16),
-    ((8, 16, 128), BF16),
-    ((8, 16, 128), BF16),
-    ((8, 96, 128), BF16),
+    ((16, 48, 128), BF16),
+    ((8, 48, 128), BF16),
+    ((8, 48, 128), BF16),
+    ((8, 32, 128), BF16),
+    ((8, 32, 128), BF16),
     ((8, 32, 128), BF16),
     ((8, 32, 128), BF16),
     ((8, 32, 128), BF16),
@@ -634,7 +702,7 @@
         in_specs=[anywhere] * 9,
         out_specs=[vmem] * 7,
         scratch_shapes=[pltpu.VMEM(s, t) for s, t in SCRATCH]
-        + [dma((n,)) for n in (9, 9, 4, 4, 12, 12, 9)],
+        + [dma((n,)) for n in (11, 9, 4, 4, 13, 13, 9)],
         compiler_params=pltpu.CompilerParams(
             collective_id=0, has_side_effects=True, vmem_limit_bytes=58 * 1024 * 1024
         ),

time: 62.4 us -> 61 us (0.978)
  Pallas kernels: 61.2 us -> 59.4 us
    pallas_call x1, Pallas kernels: 59.7 us -> 57.8 us  [shards(): pl.pallas_call(body, out_shape=[pltpu.VMEM(s, F32) for s in shapes], in_s...]
where the time goes in v2:
time: 61 us; the launch traced here: 60 us
  Pallas kernels  59.4 us (97%)
  between operations  0.64 us (1%)
    pallas_call x1, Pallas kernels, shards(): pl.pallas_call(body, out_shape=[pltpu.VMEM(s, F32) for s in shapes], in_s...  57.8 us
    pallas_call x1, Pallas kernels, shards(): pl.pallas_call(hand_over, out_shape=results, in_specs=[vmem] * 7, out_spe...  1.56 us

profile of v2, /device:TPU:6, one launch (start us, length us, event | category | flops | bytes accessed | tf_op | source)
XLA Modules:
  0.0 60.0 jit_solution(735198864583332179)
XLA Ops:
  0.6 57.8 %shard_map.144 = (f32[50,77]{1,0:T(8,128)S(1)}, f32[50,49]{1,0:T(8,128)S(1)}, f32[50,800]{1,0:T(8,128)S(1)}, f32[200,200]{1,0:T(8,128)S(1)}, f32[50,77]{1,0:T(8,...) custom-call(bf16[77,8,128]{2,1,0:T(8,128)(2,1)} %bitcast.5, bf16[77,8,128]{2,1,0:T(8,128)(2,1)} %bitcast.6, ...), custom_call_target="tpu_custom_call" | custom-call | tf_op jit(solution)/shard_map/pallas_call | solution.py:699
  58.5 1.6 %shard_map.145 = (f32[50,77]{1,0:T(8,128)}, f32[50,49]{1,0:T(8,128)}, f32[50,800]{1,0:T(8,128)}, f32[200,200]{1,0:T(8,128)}, f32[50,77]{1,0:T(8,128)}, /*index=5*/f32[1,1]{1,0:T(1,128)}, f32[616,128]{1,0:T(8,128)}) custom-call(f32[50,77]{1,0:T(8,128)S(1)} %get-tuple-element.21.refs_0_, f32[50,49]{1,0:T(8,128)S(1)} %get-tuple-element.22.refs_1_, ...), custom_call_target="tpu_custom_call" | custom-call | tf_op jit(solution)/shard_map/pallas_call | solution.py:720

commit v3 on v2

--- a/solution.py
+++ b/solution.py
@@ -15,6 +15,7 @@
 VP = 80
 C = 200
 CP = 256
+CR = 208
 FF = 800
 FP = 896
 FB = 400
@@ -217,13 +218,13 @@
     large_weights[0][1].start()
     stem_w[...] = dot(from_padded, ga[...].reshape(CP, 128)).astype(BF16)
     def stem_pair(s):
-        out = dot(stem_w[:, 0:VP], fm[:, s * LAT : (s + 2) * LAT])[0:C].astype(BF16).astype(F32)
+        out = dot(stem_w[0:CR, 0:VP], fm[:, s * LAT : (s + 2) * LAT])[0:C].astype(BF16).astype(F32)
         xs[s] = out[:, 0:LAT]
         xs[s + 1] = out[:, LAT : 2 * LAT]
 
     for s in range(HALO, HALO + COLS, 2):
         stem_pair(s)
-    kern_w = stem_w[0:208, :]
+    kern_w = stem_w[0:CR, :]
     tap_row = lax.broadcasted_iota(jnp.int32, (LAT, 2 * LAT), 0)
     second_half = (lax.broadcasted_iota(jnp.int32, (LAT, 2 * LAT), 1) >= LAT).astype(jnp.int32)
     for t in range(0, SIDE * SIDE, 2):
@@ -231,6 +232,14 @@
         taps[t] = spread[:, 0:LAT]
         if t + 1 < SIDE * SIDE:
             taps[t + 1] = spread[:, LAT : 2 * LAT]
+    def several(step):
+        def steps(group, carry):
+            for n in range(5):
+                step(group * 5 + n, carry)
+            return carry
+
+        return steps
+
     def own_taps(i):
         return [p for p in range(SIDE) if HALO <= i + 2 * p < HALO + COLS]
 
@@ -250,7 +259,7 @@
     pl.when(alone)(large_weights[1][0].start)
     large_weights[1][1].start()
     pl.when(helper)(lambda: help_on(0))
-    lax.fori_loop(0, C // 8, conv_own, 0)
+    lax.fori_loop(0, 5, several(conv_own), 0)
     pl.when(plain)(lambda: pass_on(0))
     for copy in halo:
         copy.wait_recv()
@@ -278,10 +287,10 @@
             ms[i, here, :] = out[i]
         return carry
 
-    lax.fori_loop(0, 13, conv_forward, 0)
+    lax.fori_loop(0, 3, several(conv_forward), 0)
     pl.when(helper)(lambda: help_on(1))
     pl.when(busy)(lambda: pass_on(0))
-    lax.fori_loop(13, C // 8, conv_forward, 0)
+    lax.fori_loop(3, 5, several(conv_forward), 0)
 
     nh[...] = jnp.zeros(nh.shape, BF16)
     rstds = []
@@ -301,24 +310,12 @@
     up_t[...] = second[:, 0:FP].T.astype(BF16)
     head_w[...] = second[:, FP : FP + 128]
     head_t[...] = second[:, FP : FP + 128].T.astype(BF16)
-    pl.when(plain)(lambda: pass_on(1))
+    pl.when(plain | busy)(lambda: pass_on(1))
     limits[...] = jnp.ones((1, LAT), F32)
     limits[:, 0:V] = clip[...].astype(F32) / 16.0
     sq[...] = jnp.zeros(sq.shape, F32)
     bo[...] = jnp.zeros(bo.shape, BF16)
-    for j in range(0, 2):
-        part = pl.ds(j * 2 * LAT, 2 * LAT)
-        for f in range(0, FF, FB):
-            u = dot(up_t[f : f + FB, :], nh[:, part])
-            u2 = u * u
-            half = 0.5 + 0.5 * jnp.tanh(u * (GELU_K + (GELU_K * 0.044715) * u2))
-            value = u * half
-            act[f : f + FB, part] = value.astype(BF16)
-            slope[f : f + FB, part] = half + value * (1.0 - half) * (
-                2.0 * GELU_K + (6.0 * GELU_K * 0.044715) * u2
-            )
-    pl.when(busy)(lambda: pass_on(1))
-    for j in range(2, 4):
+    for j in range(COLS // 2):
         part = pl.ds(j * 2 * LAT, 2 * LAT)
         for f in range(0, FF, FB):
             u = dot(up_t[f : f + FB, :], nh[:, part])
@@ -338,7 +335,7 @@
 
     for j in range(COLS // 2):
         part = pl.ds(j * 2 * LAT, 2 * LAT)
-        branch = dot(down_t[...], act[:, part])[0:C]
+        branch = dot(down_t[0:CR, :], act[:, part])[0:C]
         centre = jnp.concatenate([xs[HALO + 2 * j], xs[HALO + 2 * j + 1]], axis=1)
         bo[0:C, part] = (centre + branch).astype(BF16)
     for j in range(COLS // 2):
@@ -374,6 +371,7 @@
     copy_d = remote(ld.at[away], rd0, send_s.at[2], recv_s.at[2], sibling)
     copy_d.start()
     flat[...] = jnp.zeros(flat.shape, F32)
+    bh[CR:CP, :] = jnp.zeros((CP - CR, CELLS), BF16)
     stem_t[...] = stem_w[...].astype(F32).T.astype(BF16)
 
     stage_wait(0, 32, sa)
@@ -402,17 +400,17 @@
     scaled = head_s[...]
     for j in range(COLS // 2):
         part = pl.ds(j * 2 * LAT, 2 * LAT)
-        grad = dot(scaled[:, 0:VP], mis[:, part])
+        grad = dot(scaled[0:CR, 0:VP], mis[:, part])
         bg[:, part] = grad[0:C]
-        bh[:, part] = grad.astype(BF16)
+        bh[0:CR, part] = grad.astype(BF16)
     pre[FF:FP, :] = jnp.zeros((FP - FF, CELLS), BF16)
     for j in range(COLS // 2):
         part = pl.ds(j * 2 * LAT, 2 * LAT)
-        for f in range(0, FF, FB):
-            pre[f : f + FB, part] = (
-                dot(down_w[f : f + FB, :], bh[:, part]) * slope[f : f + FB, part]
+        for f in range(0, FF, 160):
+            pre[f : f + 160, part] = (
+                dot(down_w[f : f + 160, :], bh[:, part]) * slope[f : f + 160, part]
             ).astype(BF16)
-    up_grad = dot_nt(nh[...], pre[...])
+    up_grad = dot_nt(nh[0:CR, :], pre[...])
     for l in range(7):
         gup[l] = up_grad[:, 128 * l : 128 * l + 128]
     for d in range(4):
@@ -428,7 +426,7 @@
 
     for j in range(COLS // 2):
         part = pl.ds(j * 2 * LAT, 2 * LAT)
-        grad = dot(up_w[...], pre[:, part])[0:C]
+        grad = dot(up_w[0:CR, :], pre[:, part])[0:C]
         for h in range(2):
             i = 2 * j + h
             g = grad[:, h * LAT : (h + 1) * LAT]
@@ -471,12 +469,12 @@
             back[s, here, :] = out[s]
         return carry
 
-    lax.fori_loop(0, 3, conv_backward, 0)
+    lax.fori_loop(0, 1, several(conv_backward), 0)
     copy_u.wait_recv()
     for j in range(16):
         ls_u[j] = (lu[core * 16 + j].astype(F32) + ru0[j].astype(F32)).astype(BF16)
     stage(11, 16, CORES, lambda j: ls_u.at[j], rx_u.at[idx_m])
-    lax.fori_loop(3, 22, conv_backward, 0)
+    lax.fori_loop(1, 5, several(conv_backward), 0)
 
     stage_wait(7, 8, part_d)
     large = part_d[0].astype(F32)
@@ -492,7 +490,6 @@
     part_u[z] = large.astype(BF16)
     stage(5, 8, RING, lambda j: part_u.at[z], part_u.at[z])
 
-    lax.fori_loop(22, C // 8, conv_backward, 0)
     tap_col = lax.broadcasted_iota(jnp.int32, (2 * LAT, LAT), 1)
     lower_half = (lax.broadcasted_iota(jnp.int32, (2 * LAT, LAT), 0) >= LAT).astype(jnp.int32)
     kern = None
@@ -513,12 +510,11 @@
             value = value + bg[:, (s - HALO) * LAT : (s - HALO + 1) * LAT]
         sh[0:C, s * LAT : (s + 1) * LAT] = value.astype(BF16)
     small[...] = jnp.zeros(small.shape, F32)
-    small[:, 0:VP] = dot_nt(sh[...], fm[...])
+    small[0:CR, 0:VP] = dot_nt(sh[0:CR, :], fm[...])
     small[0:C, :] = small[0:C, :] + kern
-    tiny = dot(to_padded, small[...].astype(BF16))
     for j in range(8):
-        at = 64 * (j % 4) + 32 * (j // 4)
-        stx[j] = tiny[at : at + 32].astype(BF16)
+        at = 50 * (j % 4) + 32 * (j // 4)
+        stx[j] = small[at : at + 32, :].astype(BF16)
     stage(6, 8, ROW, lambda j: stx.at[j], srx.at[idx_e])
 
     for s in list(range(0, HALO, 2)) + list(range(HALO + COLS, SLOTS, 2)):
@@ -659,7 +655,7 @@
     ((C, CELLS), F32),
     ((CP, CELLS), BF16),
     ((4 * CP, 128), F32),
-    ((7, CP, 128), F32),
+    ((7, CR, 128), F32),
     ((4 * 384, 128), F32),
     ((SLOTS, C, LAT), F32),
     ((CP, SLOTS * LAT), BF16),

time: 61 us -> 59.5 us (0.975)
  Pallas kernels: 59.4 us -> 58.4 us
    pallas_call x1, Pallas kernels: 57.8 us -> 56.8 us  [shards(): pl.pallas_call(body, out_shape=[pltpu.VMEM(s, F32) for s in shapes], in_s...]
where the time goes in v3:
time: 59.5 us; the launch traced here: 59 us
  Pallas kernels  58.4 us (98%)
  between operations  0.64 us (1%)
    pallas_call x1, Pallas kernels, shards(): pl.pallas_call(body, out_shape=[pltpu.VMEM(s, F32) for s in shapes], in_s...  56.8 us
    pallas_call x1, Pallas kernels, shards(): pl.pallas_call(hand_over, out_shape=results, in_specs=[vmem] * 7, out_spe...  1.56 us

profile of v3, /device:TPU:6, one launch (start us, length us, event | category | flops | bytes accessed | tf_op | source)
XLA Modules:
  0.0 59.0 jit_solution(9170373689375905938)
XLA Ops:
  0.6 56.8 %shard_map.144 = (f32[50,77]{1,0:T(8,128)S(1)}, f32[50,49]{1,0:T(8,128)S(1)}, f32[50,800]{1,0:T(8,128)S(1)}, f32[200,200]{1,0:T(8,128)S(1)}, f32[50,77]{1,0:T(8,...) custom-call(bf16[77,8,128]{2,1,0:T(8,128)(2,1)} %bitcast.5, bf16[77,8,128]{2,1,0:T(8,128)(2,1)} %bitcast.6, ...), custom_call_target="tpu_custom_call" | custom-call | tf_op jit(solution)/shard_map/pallas_call | solution.py:695
  57.5 1.6 %shard_map.145 = (f32[50,77]{1,0:T(8,128)}, f32[50,49]{1,0:T(8,128)}, f32[50,800]{1,0:T(8,128)}, f32[200,200]{1,0:T(8,128)}, f32[50,77]{1,0:T(8,128)}, /*index=5*/f32[1,1]{1,0:T(1,128)}, f32[616,128]{1,0:T(8,128)}) custom-call(f32[50,77]{1,0:T(8,128)S(1)} %get-tuple-element.21.refs_0_, f32[50,49]{1,0:T(8,128)S(1)} %get-tuple-element.22.refs_1_, ...), custom_call_target="tpu_custom_call" | custom-call | tf_op jit(solution)/shard_map/pallas_call | solution.py:716

commit v4 on v3

--- a/solution.py
+++ b/solution.py
@@ -91,10 +91,7 @@
     idx_h = x_hi * 4 + y
     idx_e = x_hi * 4 + dp
 
-    busy = ((y == 3) & (z == 0)) | ((y == 0) & (z == 7))
-    helper = ((y == 2) & (z == 0)) | ((y == 1) & (z == 7))
-    alone, plain = jnp.logical_not(busy), jnp.logical_not(busy | helper)
-    helped = (x_hi * 32 + ((y + jnp.where(z == 0, 1, 3)) % 4) * 8 + z, dp)
+    ends = ((y == 3) & (z == 7)) | ((y == 0) & (z == 0))
 
     def peer(offset):
         a, b, c, d, e = offset
@@ -173,20 +170,11 @@
 
     for copy in halo:
         copy.start()
-    pl.when(alone)(large_weights[0][0].start)
-
-    help_copies = [
-        remote(buf.at[far], buf.at[far], send_g.at[9 + a], recv_g.at[3 + 3 * a], helped)
-        for a, buf in enumerate((gb, gd))
-    ]
+    large_weights[0][0].start()
 
     def pass_on(a):
         large_weights[a][0].wait_recv()
         large_weights[a][2].start()
-
-    def help_on(a):
-        pass_on(a)
-        help_copies[a].start()
 
     pending = []
 
@@ -256,11 +244,9 @@
                 partial[q * COLS + i, here, :] = total
         return carry
 
-    pl.when(alone)(large_weights[1][0].start)
+    large_weights[1][0].start()
     large_weights[1][1].start()
-    pl.when(helper)(lambda: help_on(0))
     lax.fori_loop(0, 5, several(conv_own), 0)
-    pl.when(plain)(lambda: pass_on(0))
     for copy in halo:
         copy.wait_recv()
     for s in list(range(0, HALO)) + list(range(HALO + COLS, SLOTS)):
@@ -287,9 +273,9 @@
             ms[i, here, :] = out[i]
         return carry
 
+    pl.when(ends)(lambda: pass_on(0))
     lax.fori_loop(0, 3, several(conv_forward), 0)
-    pl.when(helper)(lambda: help_on(1))
-    pl.when(busy)(lambda: pass_on(0))
+    pl.when(jnp.logical_not(ends))(lambda: pass_on(0))
     lax.fori_loop(3, 5, several(conv_forward), 0)
 
     nh[...] = jnp.zeros(nh.shape, BF16)
@@ -310,7 +296,7 @@
     up_t[...] = second[:, 0:FP].T.astype(BF16)
     head_w[...] = second[:, FP : FP + 128]
     head_t[...] = second[:, FP : FP + 128].T.astype(BF16)
-    pl.when(plain | busy)(lambda: pass_on(1))
+    pass_on(1)
     limits[...] = jnp.ones((1, LAT), F32)
     limits[:, 0:V] = clip[...].astype(F32) / 16.0
     sq[...] = jnp.zeros(sq.shape, F32)
@@ -583,19 +569,8 @@
             tiny = tiny + sfin[4 * h + j].astype(F32)
         o_stem[32 * h : 32 * h + rows, :] = tiny[0:rows, 0:V]
         o_kern[32 * h : 32 * h + rows, :] = pltpu.roll(tiny, LAT - V, 1)[0:rows, 0:49]
-    for copy in first_weights + halo + [large_weights[a][i] for a in (0, 1) for i in (1, 2)]:
+    for copy in first_weights + halo + list(large_weights[0] + large_weights[1]):
         copy.wait_send()
-
-    @pl.when(alone)
-    def _():
-        large_weights[0][0].wait_send()
-        large_weights[1][0].wait_send()
-
-    @pl.when(helper)
-    def _():
-        help_copies[0].wait_send()
-        help_copies[1].wait_send()
-
     for copy in [copy_d, copy_u, copy_l, copy_r] + pending:
         copy.wait_send()
 
@@ -698,7 +673,7 @@
         in_specs=[anywhere] * 9,
         out_specs=[vmem] * 7,
         scratch_shapes=[pltpu.VMEM(s, t) for s, t in SCRATCH]
-        + [dma((n,)) for n in (11, 9, 4, 4, 13, 13, 9)],
+        + [dma((n,)) for n in (9, 9, 4, 4, 13, 13, 9)],
         compiler_params=pltpu.CompilerParams(
             collective_id=0, has_side_effects=True, vmem_limit_bytes=58 * 1024 * 1024
         ),

time: 59.5 us -> 58 us (0.975)
  Pallas kernels: 58.4 us -> 56.8 us
    pallas_call x1, Pallas kernels: 56.8 us -> 55.3 us  [shards(): pl.pallas_call(body, out_shape=[pltpu.VMEM(s, F32) for s in shapes], in_s...]
where the time goes in v4:
time: 58 us; the launch traced here: 57.5 us
  Pallas kernels  56.8 us (98%)
  between operations  0.64 us (1%)
    pallas_call x1, Pallas kernels, shards(): pl.pallas_call(body, out_shape=[pltpu.VMEM(s, F32) for s in shapes], in_s...  55.3 us
    pallas_call x1, Pallas kernels, shards(): pl.pallas_call(hand_over, out_shape=results, in_specs=[vmem] * 7, out_spe...  1.56 us

profile of v4, /device:TPU:6, one launch (start us, length us, event | category | flops | bytes accessed | tf_op | source)
XLA Modules:
  0.0 57.5 jit_solution(17913217930809377317)
XLA Ops:
  0.6 55.3 %shard_map.144 = (f32[50,77]{1,0:T(8,128)S(1)}, f32[50,49]{1,0:T(8,128)S(1)}, f32[50,800]{1,0:T(8,128)S(1)}, f32[200,200]{1,0:T(8,128)S(1)}, f32[50,77]{1,0:T(8,...) custom-call(bf16[77,8,128]{2,1,0:T(8,128)(2,1)} %bitcast.5, bf16[77,8,128]{2,1,0:T(8,128)(2,1)} %bitcast.6, ...), custom_call_target="tpu_custom_call" | custom-call | tf_op jit(solution)/shard_map/pallas_call | solution.py:670
  55.9 1.6 %shard_map.145 = (f32[50,77]{1,0:T(8,128)}, f32[50,49]{1,0:T(8,128)}, f32[50,800]{1,0:T(8,128)}, f32[200,200]{1,0:T(8,128)}, f32[50,77]{1,0:T(8,128)}, /*index=5*/f32[1,1]{1,0:T(1,128)}, f32[616,128]{1,0:T(8,128)}) custom-call(f32[50,77]{1,0:T(8,128)S(1)} %get-tuple-element.21.refs_0_, f32[50,49]{1,0:T(8,128)S(1)} %get-tuple-element.22.refs_1_, ...), custom_call_target="tpu_custom_call" | custom-call | tf_op jit(solution)/shard_map/pallas_call | solution.py:691
